TPU v7x, 128 devices: a whole 4x4x4 slice. The times are simulated.
128 devices in a mesh: dp: 8 (over x, z_hi), ctx: 16 (over z_lo, y, core).
Axes of the slice: x: 4, y: 4, z: 4 (z_hi: 2, z_lo: 2; z = z_hi * 2 + z_lo), core: 2. Of those that a mesh axis runs over, the one named last changes fastest.
Arguments:
- events: bfloat16 [8, 4096, 512], P('dp', 'ctx'), may hold values from -6 to 6
- upstream: bfloat16 [8, 4096, 512], P('dp', 'ctx'), may hold values from -6 to 6
- lengths: int32 [8], P('dp'), may hold values from 1024 to 4096, as said below
- block_slots: int32 [32], replicated, may hold values from 0 to 31, as said below
- pattern: int32 [32, 3], replicated, may hold values from 0 to 31, as said below
- in_weight: bfloat16 [512, 2048], replicated, may hold values from -0.25 to 0.25
- out_weight: bfloat16 [512, 512], replicated, may hold values from -0.25 to 0.25
Outputs:
- encoded: bfloat16 [8, 4096, 512], P('dp', 'ctx')
- grad_events: bfloat16 [8, 4096, 512], P('dp', 'ctx')
- grad_in_weight: float32 [512, 2048], replicated
- grad_out_weight: float32 [512, 512], replicated
Inputs may be any that keep to these rules, and one draw needn't show every extreme that they name: `lengths`: the first user's history fills all 4096 positions. A permutation: slot s of context device c holds history block block_slots[c * 2 + s]. `pattern`: every entry of row b is at most b, and row 0 is all zeros; entries may repeat; the query blocks held by one context device read at most 2 distinct key blocks held by any one other context device, and exactly 2 for some pair of devices.
All inputs are finite; a program needn't handle non-finite values.
Results may differ from a plain program's by a relative error of at most 0.012.
Values may be sent and summed in bfloat16 or wider, within the bound.
A program may use at most 128 MiB of HBM per device.

v0:
```python
import jax
import jax.numpy as jnp
from jax import lax
from jax.sharding import PartitionSpec as P

HEADS = 4
HD = 128
BLK = 128
KSEL = 4
KEYS = 512


eps_norm = 1e-05


def silu_slope(value):
    sigma = jax.nn.sigmoid(value)
    return sigma * (1.0 + value * (1.0 - sigma))


def norm_rows(value):
    centre = value - jnp.mean(value, axis=-1, keepdims=True)
    inverse = lax.rsqrt(jnp.mean(centre * centre, axis=-1, keepdims=True) + eps_norm)
    return (centre * inverse, inverse)


def norm_back(grad_hat, normal, inverse):
    return inverse * (
        grad_hat
        - jnp.mean(grad_hat, -1, keepdims=True)
        - normal * jnp.mean(grad_hat * normal, -1, keepdims=True)
    )


def slot_table(block_slots, blocks):
    store = jnp.arange(blocks, dtype=jnp.int32)
    return jnp.sum(
        store[None, :] * (block_slots[None, :] == store[:, None]).astype(jnp.int32), axis=1
    )


def block_plan(block_slots, pattern, length, query_slots, blocks):
    slot_of = slot_table(block_slots, blocks)
    global_q = block_slots[query_slots]
    listed = jnp.concatenate([global_q[:, None], pattern[global_q]], axis=1)
    same = listed[:, :, None] == listed[:, None, :]
    earlier = jnp.arange(KSEL)[None, :] < jnp.arange(KSEL)[:, None]
    fresh = jnp.logical_not(jnp.any(same & earlier[None], axis=2))
    offsets = jnp.arange(BLK, dtype=jnp.int32)
    q_pos = global_q[:, None] * BLK + offsets[None, :]
    k_pos = (listed[:, :, None] * BLK + offsets[None, None, :]).reshape(
        query_slots.shape[0], KSEL * BLK
    )
    k_live = jnp.repeat(fresh, BLK, axis=1) & (k_pos < length)
    mask = (
        k_live[:, None, :] & (k_pos[:, None, :] <= q_pos[:, :, None]) & (q_pos < length)[:, :, None]
    )
    return (slot_of[listed], mask.astype(jnp.float32))


def local(events, upstream, lengths, block_slots, pattern, in_weight, out_weight):
    f32 = jnp.float32
    bf16 = jnp.bfloat16
    scale = HD ** (-0.5)
    history = events[0]
    grad_top = upstream[0]
    length = lengths[0]
    rows, width = history.shape
    per_dev = rows // BLK
    blocks = block_slots.shape[0]
    here = lax.axis_index("ctx")
    hat_in, inv_in = norm_rows(history.astype(f32))
    normed = hat_in.astype(bf16)
    preact = jnp.dot(normed, in_weight, preferred_element_type=f32)
    active = jax.nn.silu(preact).astype(bf16)
    feat_u = active[:, :width]
    feat_v = active[:, width : 2 * width]
    feat_q = active[:, 2 * width : 3 * width]
    feat_k = active[:, 3 * width :]
    query_slots = here * per_dev + jnp.arange(per_dev, dtype=jnp.int32)
    key_store, mask = block_plan(block_slots, pattern, length, query_slots, blocks)
    source = jnp.concatenate([feat_k, feat_v], axis=1)
    fetch_width = source.shape[1]
    whole = lax.all_gather(source, "ctx", axis=0, tiled=True)
    picked = whole.reshape(blocks, BLK, fetch_width)[key_store].reshape(per_dev * KEYS, fetch_width)
    k_sel = picked[:, :width].reshape(per_dev, KEYS, HEADS, HD)
    v_sel = picked[:, width:].reshape(per_dev, KEYS, HEADS, HD)
    q_blk = feat_q.reshape(per_dev, BLK, HEADS, HD)
    scores = jnp.einsum("bihd,bjhd->bhij", q_blk, k_sel, preferred_element_type=f32) * scale
    weights = (jax.nn.silu(scores) * mask[:, None]).astype(bf16)
    mixed = jnp.einsum("bhij,bjhd->bihd", weights, v_sel, preferred_element_type=f32).reshape(
        rows, width
    )
    hat_mix, inv_mix = norm_rows(mixed)
    gated = (hat_mix * feat_u.astype(f32)).astype(bf16)
    encoded = (history.astype(f32) + jnp.dot(gated, out_weight, preferred_element_type=f32)).astype(
        bf16
    )
    grad_gated = jnp.dot(grad_top, out_weight.T, preferred_element_type=f32)
    grad_out = jnp.dot(gated.T, grad_top, preferred_element_type=f32)
    grad_u = grad_gated * hat_mix
    grad_mixed = norm_back(grad_gated * feat_u.astype(f32), hat_mix, inv_mix).astype(bf16)
    grad_mh = grad_mixed.reshape(per_dev, BLK, HEADS, HD)
    grad_weights = jnp.einsum("bihd,bjhd->bhij", grad_mh, v_sel, preferred_element_type=f32)
    grad_scores = (grad_weights * silu_slope(scores) * mask[:, None] * scale).astype(bf16)
    grad_q = jnp.einsum("bhij,bjhd->bihd", grad_scores, k_sel, preferred_element_type=f32).reshape(
        rows, width
    )
    grad_k_sel = jnp.einsum(
        "bhij,bihd->bjhd", grad_scores, q_blk, preferred_element_type=f32
    ).reshape(per_dev * KSEL, BLK, width)
    grad_v_sel = jnp.einsum(
        "bhij,bihd->bjhd", weights, grad_mh, preferred_element_type=f32
    ).reshape(per_dev * KSEL, BLK, width)
    index = key_store.reshape(-1)
    spread_k = (
        jnp.zeros((blocks, BLK, width), f32).at[index].add(grad_k_sel).reshape(blocks * BLK, width)
    )
    spread_v = (
        jnp.zeros((blocks, BLK, width), f32).at[index].add(grad_v_sel).reshape(blocks * BLK, width)
    )
    grad_k, grad_v = (
        lax.psum_scatter(
            spread_k.astype(jnp.bfloat16), "ctx", scatter_dimension=0, tiled=True
        ).astype(jnp.float32),
        lax.psum_scatter(
            spread_v.astype(jnp.bfloat16), "ctx", scatter_dimension=0, tiled=True
        ).astype(jnp.float32),
    )
    grad_act = jnp.concatenate([grad_u, grad_v, grad_q, grad_k], axis=1)
    grad_pre = (grad_act * silu_slope(preact)).astype(bf16)
    grad_in = jnp.dot(normed.T, grad_pre, preferred_element_type=f32)
    grad_normed = jnp.dot(grad_pre, in_weight.T, preferred_element_type=f32)
    grad_events = (grad_top.astype(f32) + norm_back(grad_normed, hat_in, inv_in)).astype(bf16)
    grad_in, grad_out = lax.psum((grad_in, grad_out), ("dp", "ctx"))
    return (encoded[None], grad_events[None], grad_in, grad_out)


def solution(mesh):
    return jax.shard_map(
        local,
        mesh=mesh,
        in_specs=(P("dp", "ctx", None), P("dp", "ctx", None), P("dp"), P(), P(), P(), P()),
        out_specs=(P("dp", "ctx", None), P("dp", "ctx", None), P(), P()),
        check_vma=False,
    )
```

profile of v0, /device:TPU:1, one launch (start us, length us, event | category | flops | bytes accessed | tf_op | source)
XLA Modules:
  0.0 431.6 jit_solution(13654828368566421925)
XLA Ops:
  7.2 1.2 convert_reduce_fusion
  8.4 1.2 fusion.16
  9.6 3.1 multiply_convert_fusion.2
  12.7 1.0 copy-done.7
  13.8 0.9 pad_maximum_fusion
  15.4 0.6 gather_fusion
  16.3 0.6 gather_fusion.1
  17.5 0.6 gather_fusion.2
  19.1 51.5 %all-gather.2.cloned.1.call-done = bf16[4096,1024]{1,0:T(8,128)(2,1)} async-done(((bf16[256,1024]{1,0:T(8,128)(2,1)}), bf16[4096,1024]{1,0:T(8,128)(2,1)}) %all-gather.2.cloned.1.call-update) | async-done | bytes 8388624 | tf_op jit(solution)/shard_map/all_gather | solution.py:84
  70.6 5.4 %gather_fusion.3 = bf16[8,128,1024]{2,1,0:T(8,128)(2,1)} fusion(bf16[32,128,1024]{2,1,0:T(8,128)(2,1)} %bitcast.138, s32[1024]{0:T(1024)S(1)} %pad_clamp_fusion), kind=kCustom, calls=%fused_computation.3 | custom fusion | bytes 4194336 | tf_op jit(solution)/shard_map/gather | solution.py:85
  76.0 3.0 fusion.41
  79.0 2.1 reshape.383
  81.1 2.1 reshape.385
  83.3 2.4 copy.48
  85.7 3.4 multiply_convert_fusion.1
  90.5 1.6 fusion.26
  92.1 2.0 fusion.38
  94.2 3.2 multiply_convert_fusion
  97.3 1.0 copy-done.6
  98.3 1.7 convolution_bitcast_fusion
  100.1 2.9 copy.51
  103.0 3.0 reshape.437
  106.0 4.3 broadcast.288.clone
  110.3 5.1 %scatter_fusion.1 = f32[32,128,512]{2,1,0:T(8,128)} fusion(f32[32,128,512]{2,1,0:T(8,128)} %broadcast.288.clone, s32[8]{0:T(128)S(1)} %fusion.29, f32[8,128,512]{2,1,0:T(8,128)} %reshape.437), kind=kCustom, calls=%fused_computation.5 | custom fusion | flops 524288 | bytes 6291488 | tf_op jit(solution)/shard_map/scatter-add | solution.py:117
  115.5 6.0 %convert_element_type.82 = bf16[32,128,512]{2,1,0:T(8,128)(2,1)} convert(f32[32,128,512]{2,1,0:T(8,128)} %scatter_fusion.1) | non-fusion elementwise | flops 2097152 | bytes 12582912 | tf_op jit(solution)/shard_map/convert_element_type | solution.py:124
  121.8 3.1 convolution_bitcast_fusion.1
  124.8 2.9 copy.45
  127.7 3.1 reshape.429
  130.7 4.3 broadcast.288.clone.1
  135.0 5.2 %scatter_fusion = f32[32,128,512]{2,1,0:T(8,128)} fusion(f32[32,128,512]{2,1,0:T(8,128)} %broadcast.288.clone.1, s32[8]{0:T(128)S(1)} %fusion.29, f32[8,128,512]{2,1,0:T(8,128)} %reshape.429), kind=kCustom, calls=%fused_computation.4 | custom fusion | flops 524288 | bytes 6291488 | tf_op jit(solution)/shard_map/scatter-add | solution.py:120
  140.2 6.0 %convert_element_type.78 = bf16[32,128,512]{2,1,0:T(8,128)(2,1)} convert(f32[32,128,512]{2,1,0:T(8,128)} %scatter_fusion) | non-fusion elementwise | flops 2097152 | bytes 12582912 | tf_op jit(solution)/shard_map/convert_element_type | solution.py:127
  146.3 2.0 convolution_bitcast_fusion.2
  148.3 1.0 copy.49
  149.3 1.9 copy.83
  151.2 2.4 fusion.20
  153.6 31.2 %reduce-scatter.5.cloned.1.call-done = bf16[256,512]{1,0:T(8,128)(2,1)} async-done(((bf16[4096,512]{1,0:T(8,128)(2,1)}), bf16[256,512]{1,0:T(8,128)(2,1)}) %reduce-scatter.5.cloned.1.call-update) | async-done | bytes 262160 | tf_op jit(solution)/shard_map/reduce_scatter | solution.py:123
  184.8 1.8 convert_element_type.84
  186.6 65.9 %reduce-scatter.3.cloned.1.call-done = bf16[256,512]{1,0:T(8,128)(2,1)} async-done(((bf16[4096,512]{1,0:T(8,128)(2,1)}), bf16[256,512]{1,0:T(8,128)(2,1)}) %reduce-scatter.3.cloned.1.call-update) | async-done | bytes 262160 | tf_op jit(solution)/shard_map/reduce_scatter | solution.py:126
  252.5 1.0 convert_element_type.80
  253.5 2.9 fusion
  256.4 1.0 copy-done.3
  257.4 2.9 fusion.31
  260.3 2.2 fusion.2
  262.5 2.1 fusion.40
  264.6 1.0 fusion.19
  265.5 153.8 %all-reduce.3.cloned.1.call-done = (f32[512,2048]{1,0:T(8,128)}, f32[512,512]{1,0:T(8,128)}) async-done(((f32[512,2048]{1,0:T(8,128)}, f32[512,512]{1,0:T(8,128)}), (f32[512,2048]{1,0:T(8,128)}, f32[512,512]{1,0:T(8,128)})) %all-reduce.3.cloned.1.call-update) | async-done | bytes 5242896 | tf_op jit(solution)/shard_map/psum | solution.py:135
  419.3 4.8 %copy.89 = f32[512,2048]{1,0:T(8,128)} copy(f32[512,2048]{1,0:T(8,128)} %get-tuple-element.35) | data formatting | bytes 8388608
  424.1 1.0 copy.90
  (75 shorter events, 3.8 us)
Async XLA Ops:
  7.2 2.5 copy-start
  7.2 63.5 %all-gather.2.cloned.1.call-start = ((), (), s32[]{:S(2)}) async-start(), calls=%async_computation.2 | async-start | bytes 8912896 | tf_op jit(solution)/shard_map/all_gather | solution.py:84
  12.7 1.0 copy-start.7
  12.7 2.7 copy-start.1
  12.7 3.5 copy-start.13
  14.7 170.2 %reduce-scatter.5.cloned.1.call-start = ((), (), s32[]{:S(2)}) async-start(), calls=%async_computation.4 | async-start | bytes 4456448 | tf_op jit(solution)/shard_map/reduce_scatter | solution.py:123
  18.6 67.1 %copy-start.10 = (bf16[2,128,4,128]{1,3,2,0:T(8,128)(2,1)}, bf16[2,128,4,128]{1,3,2,0:T(8,128)(2,1)S(1)}, u32[]{:S(2)}) copy-start(bf16[2,128,4,128]{1,3,2,0:T(8,128)(2,1)S(1)} %copy.50) | copy-start | bytes 786436
  19.1 66.6 %copy-start.12 = (f32[2,128,512]{2,1,0:T(8,128)}, f32[2,128,512]{2,1,0:T(8,128)S(1)}, u32[]{:S(2)}) copy-start(f32[2,128,512]{2,1,0:T(8,128)S(1)} %and_convert_fusion) | copy-start | bytes 1572868
  85.7 3.4 copy-start.5
  89.1 1.1 copy-start.4
  89.1 1.4 copy-start.8
  94.1 4.2 copy-start.11
  97.3 1.0 copy-start.6
  121.5 131.0 %reduce-scatter.3.cloned.1.call-start = ((), (), s32[]{:S(2)}) async-start(), calls=%async_computation.3 | async-start | bytes 4456448 | tf_op jit(solution)/shard_map/reduce_scatter | solution.py:126
  146.2 273.1 %all-reduce.3.cloned.1.call-start = ((), (), s32[]{:S(2)}) async-start(), calls=%async_computation.5 | async-start | bytes 10485760 | tf_op jit(solution)/shard_map/psum | solution.py:135
  253.5 3.9 copy-start.2
  256.4 1.0 copy-start.3
  419.3 4.8 %copy-start.9 = (f32[512,512]{1,0:T(8,128)S(1)}, f32[512,512]{1,0:T(8,128)}, u32[]{:S(2)}) copy-start(f32[512,512]{1,0:T(8,128)} %get-tuple-element.36) | copy-start | bytes 3145732
Sparse Core Ops, SparseCore 0:
  14.8 55.8 all-gather.1
  121.6 63.1 reduce-scatter.4
  187.2 65.2 reduce-scatter.2
  260.4 158.8 all-reduce.2
where the time goes:
time: 432 us
  waiting for transfers between devices  302 us (70%)
  local copies, waits for them, and re-layouts  50.9 us (12%)
  other arithmetic  35.1 us (8%)
  matrix products  28 us (6%)
  between operations  14.7 us (3%)
    psum x1, waiting for transfers between devices, local(): grad_in, grad_out = lax.psum((grad_in, grad_out), ('dp', 'ctx'))  154 us
    reduce_scatter x1, waiting for transfers between devices, local(): lax.psum_scatter(spread_v.astype(jnp.bfloat16), 'ctx', scatter_dimension=...  65.9 us
    all_gather x1, waiting for transfers between devices, local(): whole = lax.all_gather(source, 'ctx', axis=0, tiled=True)  51.5 us
    reduce_scatter x1, waiting for transfers between devices, local(): lax.psum_scatter(spread_k.astype(jnp.bfloat16), 'ctx', scatter_dimension=...  31.2 us
    unnamed x34, local copies, waits for them, and re-layouts  11.4 us
  transfers between devices with their start and end apart: 4, of which 4 were waited for; matrix products, arithmetic and copies ran while one was open for 10% of the time, Pallas kernels for 0%

commit v1 on v0

v1 whole, which is shorter than its diff:
```python
import functools

import jax
import jax.numpy as jnp
from jax import lax
from jax.experimental import pallas as pl
from jax.experimental.pallas import tpu as pltpu
from jax.sharding import PartitionSpec as P

HEADS = 4
HD = 128
BLK = 128
D = 512
EPS = 1e-05
SCALE = HD ** (-0.5)
MESH = pl.DeviceIdType.MESH
F32 = jnp.float32
BF16 = jnp.bfloat16
FAR = 1 << 20
G_OUT, G_U, G_Q, G_V, G_K = 0, 512, 1024, 1536, 2048
GCOLS = 2560
N_SEM = 96


def dot(a, b):
    return jnp.dot(a, b, preferred_element_type=F32)


def dot_nt(a, b):
    return lax.dot_general(a, b, (((1,), (1,)), ((), ())), preferred_element_type=F32)


def dot_tn(a, b):
    return lax.dot_general(a, b, (((0,), (0,)), ((), ())), preferred_element_type=F32)


def sigmoid(z):
    return 0.5 + 0.5 * jnp.tanh(0.5 * z)


def norm_rows(z):
    centre = z - jnp.mean(z, axis=-1, keepdims=True)
    inverse = lax.rsqrt(jnp.mean(centre * centre, axis=-1, keepdims=True) + EPS)
    return centre * inverse, inverse


def norm_back(grad, hat, inverse):
    return inverse * (
        grad
        - jnp.mean(grad, axis=-1, keepdims=True)
        - hat * jnp.mean(grad * hat, axis=-1, keepdims=True)
    )


class Net:
    def __init__(self, send_sems, recv_sems):
        self.send_sems, self.recv_sems = send_sems, recv_sems
        self.copies = []

    def send(self, src, dst, device):
        at = len(self.copies)
        copy = pltpu.make_async_remote_copy(
            src_ref=src,
            dst_ref=dst,
            send_sem=self.send_sems.at[at],
            recv_sem=self.recv_sems.at[at],
            device_id=device,
            device_id_type=MESH,
        )
        copy.start()
        self.copies.append((copy, device))
        return at

    def landed(self, at, ref):
        pltpu.make_async_remote_copy(
            src_ref=ref,
            dst_ref=ref,
            send_sem=self.send_sems.at[at],
            recv_sem=self.recv_sems.at[at],
            device_id=self.copies[at][1],
            device_id_type=MESH,
        ).wait_recv()

    def drain(self):
        for copy, _ in self.copies:
            copy.wait_send()


def layer_kernel(
    slots_ref, pattern_ref, length_ref, events, upstream, w_hbm, wo_hbm,
    encoded, grad_events, gw,
    w, wo, gx, normed, own_normed, hat_in, inv_in,
    u_act, u_slope, q_act, q_slope, k_act, k_slope, v_act, v_slope,
    grad_gated, limit_mask, weights, slope, mixed, grad_mixed, grad_q,
    dv, dk, own_grad, compact,
    to_sib, from_sib, sum_y, sum_z, r_z2, r_ya, r_yb, r_h, r_p, r_m, r_z0,
    gp, g_sib, g_x, g_z, g_y, g_zs,
    w_sems, send_sems, recv_sems,
):
    dp = lax.axis_index("dp")
    ctx = lax.axis_index("ctx")
    x, zh = dp // 2, dp % 2
    zl, y, core = ctx // 8, (ctx // 2) % 4, ctx % 2
    z = zh * 2 + zl

    def dev(x, y, z, core):
        return {"dp": x * 2 + z // 2, "ctx": ((z % 2) * 4 + y) * 2 + core}

    def rot(v, by):
        return lax.rem(v + by, 4)

    sib = dev(x, y, z, 1 - core)
    yp, ym, y2 = (dev(x, rot(y, i), z, core) for i in (1, 3, 2))
    zp = dev(x, y, zh * 2 + 1 - zl, core)
    ring_x = [dev(rot(x, i), y, z, core) for i in range(4)]
    ring_y = [dev(x, rot(y, i), z, core) for i in range(4)]
    ring_z = [dev(x, y, rot(z, i), core) for i in range(4)]

    w_copy = pltpu.make_async_copy(w_hbm, w, w_sems.at[0])
    wo_copy = pltpu.make_async_copy(wo_hbm, wo, w_sems.at[1])
    w_copy.start()
    wo_copy.start()

    barrier = pltpu.get_barrier_semaphore()
    partners = [sib] + ring_x[1:] + ring_y[1:] + ring_z[1:]
    for partner in partners:
        pl.semaphore_signal(barrier, inc=1, device_id=partner, device_id_type=MESH)

    net = Net(send_sems, recv_sems)

    def shard(dz, dy, side):
        zz = zl if dz == 0 else 1 - zl
        kk = core if side == 0 else 1 - core
        return ((zz * 4 + rot(y, dy)) * 2 + kk) * 2

    def rows(dz, dy, side=0, half=None):
        base = shard(dz, dy, side)
        if half is None:
            return gx.at[pl.ds(base, 2)]
        return gx.at[base + half]

    for half in range(2):
        gx[shard(0, 0, 0) + half] = events[half * 128 : half * 128 + 128, :]
    pl.semaphore_wait(barrier, len(partners))

    def forward(ref, device):
        return net.send(ref, ref, device)

    a_yp0 = forward(rows(0, 0, 0, 0), yp)
    a_ym0 = forward(rows(0, 0, 0, 1), ym)
    a_z0 = forward(rows(0, 0, 0, 0), zp)
    a_sib = forward(rows(0, 0), sib)
    a_yp1 = forward(rows(0, 0, 0, 1), yp)
    a_ym1 = forward(rows(0, 0, 0, 0), ym)
    a_z1 = forward(rows(0, 0, 0, 1), zp)

    hat, inv = norm_rows(events[...].astype(F32))
    hat_in[...] = hat
    inv_in[...] = inv
    own = hat.astype(BF16)
    own_normed[...] = own
    for b in range(2):
        normed[b * 512 : b * 512 + 128, :] = own[b * 128 : b * 128 + 128]
    w_copy.wait()
    wo_copy.wait()

    def activate(pre):
        sig = sigmoid(pre)
        act = pre * sig
        return act.astype(BF16), sig + act * (1.0 - sig)

    for h in range(4):
        act, sl = activate(dot(own_normed[...], w[:, h * 128 : h * 128 + 128]))
        u_act[h] = act
        u_slope[h] = sl
        act, sl = activate(dot(own_normed[...], w[:, 1024 + h * 128 : 1152 + h * 128]))
        q_act[h] = act
        q_slope[h] = sl

    net.landed(a_yp0, rows(0, 3, 0, 0))
    r_yp = forward(rows(0, 3, 0, 0), yp)
    net.landed(a_ym0, rows(0, 1, 0, 1))
    r_ym = forward(rows(0, 1, 0, 1), ym)
    net.landed(a_z0, rows(1, 0, 0, 0))
    f_yp0 = forward(rows(1, 0, 0, 0), yp)
    f_ym0 = forward(rows(1, 0, 0, 0), ym)

    for h in range(4):
        grad_gated[h] = dot_nt(upstream[...], wo[h * 128 : h * 128 + 128, :])

    def project(lo, n):
        for h in range(4):
            act, sl = activate(dot(normed[pl.ds(lo, n), :], w[:, 512 + h * 128 : 640 + h * 128]))
            v_act[h, pl.ds(lo, n), :] = act
            v_slope[h, pl.ds(lo, n), :] = sl
            act, sl = activate(dot(normed[pl.ds(lo, n), :], w[:, 1536 + h * 128 : 1664 + h * 128]))
            k_act[h, pl.ds(lo, n), :] = act
            k_slope[h, pl.ds(lo, n), :] = sl

    net.landed(a_yp1, rows(0, 3, 0, 1))
    d1 = forward(rows(0, 3), sib)
    net.landed(a_ym1, rows(0, 1, 0, 0))
    d2 = forward(rows(0, 1), sib)
    net.landed(a_z1, rows(1, 0, 0, 1))
    f_yp1 = forward(rows(1, 0, 0, 1), yp)
    f_ym1 = forward(rows(1, 0, 0, 1), ym)
    d3 = forward(rows(1, 0), sib)
    project(0, 128)
    project(512, 128)
    net.landed(r_yp, rows(0, 2, 0, 0))
    z2_0 = forward(rows(0, 2, 0, 0), zp)
    net.landed(r_ym, rows(0, 2, 0, 1))
    z2_1 = forward(rows(0, 2, 0, 1), zp)
    d4 = forward(rows(0, 2), sib)

    length = length_ref[0]
    listed, at_slot, fresh = [], [], []
    for b in range(2):
        mine = slots_ref[2 * ctx + b]
        picks = [mine] + [pattern_ref[mine, t] for t in range(3)]
        listed.append(picks)
        news = [None]
        for t in range(1, 4):
            new = picks[t] != picks[0]
            for s in range(1, t):
                new = jnp.logical_and(new, picks[t] != picks[s])
            news.append(new)
        fresh.append(news)
    found = [[jnp.int32(0)] * 4 for _ in range(2)]
    for s in range(32):
        block = slots_ref[s]
        for b in range(2):
            for t in range(1, 4):
                found[b][t] = jnp.where(block == listed[b][t], s, found[b][t])

    for b in range(2):
        q_pos = listed[b][0] * 128 + lax.broadcasted_iota(jnp.int32, (128, 128), 0)
        top = jnp.where(q_pos < length, q_pos, -1)
        lane = lax.broadcasted_iota(jnp.int32, (128, 128), 1)
        for t in range(4):
            start = listed[b][t] * 128
            if t:
                start = jnp.where(fresh[b][t], start, FAR)
            limit_mask[b, :, t * 128 : t * 128 + 128] = (start + lane <= top).astype(F32)

    net.landed(f_yp0, rows(1, 3, 0, 0))
    net.landed(f_yp1, rows(1, 3, 0, 1))
    d5 = forward(rows(1, 3), sib)
    net.landed(f_ym0, rows(1, 1, 0, 0))
    net.landed(f_ym1, rows(1, 1, 0, 1))
    d6 = forward(rows(1, 1), sib)
    net.landed(z2_0, rows(1, 2, 0, 0))
    net.landed(z2_1, rows(1, 2, 0, 1))
    d7 = forward(rows(1, 2), sib)
    for at, (dz, dy) in zip(
        (a_sib, d1, d2, d3, d4, d5, d6, d7),
        ((0, 0), (0, 3), (0, 1), (1, 0), (0, 2), (1, 3), (1, 1), (1, 2)),
    ):
        net.landed(at, rows(dz, dy, 1))

    for b in range(2):
        for t in range(1, 4):
            block = gx[found[b][t]]
            normed[b * 512 + t * 128 : b * 512 + t * 128 + 128, :] = norm_rows(block.astype(F32))[
                0
            ].astype(BF16)
    project(128, 384)
    project(640, 384)

    def forward_head(i, carry):
        b, h = i // 4, i % 4
        q = q_act[h, pl.ds(pl.multiple_of(b * 128, 128), 128), :]
        for t in range(4):
            lo = pl.multiple_of(b * 512 + t * 128, 128)
            s = dot_nt(q, k_act[h, pl.ds(lo, 128), :]) * SCALE
            mask = limit_mask[b, :, t * 128 : t * 128 + 128]
            sig = sigmoid(s)
            act = s * sig
            weights[i, :, t * 128 : t * 128 + 128] = (act * mask).astype(BF16)
            slope[i, :, t * 128 : t * 128 + 128] = (sig + act * (1.0 - sig)) * (mask * SCALE)
        mixed[h, pl.ds(pl.multiple_of(b * 128, 128), 128), :] = dot(
            weights[i], v_act[h, pl.ds(pl.multiple_of(b * 512, 512), 512), :]
        )
        return carry

    lax.fori_loop(0, 8, forward_head, 0)

    def across(parts):
        return sum(jnp.sum(part, axis=-1, keepdims=True) for part in parts) * (1.0 / D)

    parts = [mixed[h] for h in range(4)]
    mean = across(parts)
    parts = [part - mean for part in parts]
    inv_mix = lax.rsqrt(across([part * part for part in parts]) + EPS)
    hats = [part * inv_mix for part in parts]
    us = [u_act[h].astype(F32) for h in range(4)]
    gated = jnp.concatenate([(hats[h] * us[h]).astype(BF16) for h in range(4)], axis=1)
    encoded[...] = (events[...].astype(F32) + dot(gated, wo[...])).astype(BF16)
    gp[:, G_OUT : G_OUT + 512] = dot_tn(gated, upstream[...]).astype(BF16)
    ggs = [grad_gated[h] for h in range(4)]
    du = jnp.concatenate([(ggs[h] * hats[h] * u_slope[h]).astype(BF16) for h in range(4)], axis=1)
    gp[:, G_U : G_U + 512] = dot_tn(own_normed[...], du).astype(BF16)
    own_grad[...] = dot_nt(du, w[:, 0:512])
    ts = [ggs[h] * us[h] for h in range(4)]
    mean_t = across(ts)
    mean_th = across([ts[h] * hats[h] for h in range(4)])
    for h in range(4):
        grad_mixed[h] = (inv_mix * (ts[h] - mean_t - hats[h] * mean_th)).astype(BF16)

    def backward_head(i, carry):
        b, h = i // 4, i % 4
        q_rows = pl.ds(pl.multiple_of(b * 128, 128), 128)
        k_rows = pl.ds(pl.multiple_of(b * 512, 512), 512)
        gm = grad_mixed[h, q_rows, :]
        q = q_act[h, q_rows, :]
        gs = (dot_nt(gm, v_act[h, k_rows, :]) * slope[i]).astype(BF16)
        grad_q[h, q_rows, :] = dot(gs, k_act[h, k_rows, :])
        dk[h, k_rows, :] = (dot_tn(gs, q) * k_slope[h, k_rows, :]).astype(BF16)
        dv[h, k_rows, :] = (dot_tn(weights[i], gm) * v_slope[h, k_rows, :]).astype(BF16)
        return carry

    lax.fori_loop(0, 8, backward_head, 0)

    dv_all = jnp.concatenate([dv[h] for h in range(4)], axis=1)
    dk_all = jnp.concatenate([dk[h] for h in range(4)], axis=1)
    back = dot_nt(dv_all, w[:, 512:1024]) + dot_nt(dk_all, w[:, 1536:2048])
    for b in range(2):
        for t in range(1, 4):
            lo = b * 512 + t * 128
            compact[b * 3 + t - 1] = back[lo : lo + 128].astype(BF16)
        own_grad[b * 128 : b * 128 + 128, :] += back[b * 512 : b * 512 + 128]
    compact[6] = jnp.zeros((128, 512), BF16)

    def pieces(dz, dy, side):
        zz = zl if dz == 0 else 1 - zl
        kk = core if side == 0 else 1 - core
        base = ((zz * 4 + rot(y, dy)) * 2 + kk) * 2
        out = []
        for i in range(2):
            total = []
            for b in range(2):
                at = jnp.int32(6)
                for t in range(1, 4):
                    hit = jnp.logical_and(found[b][t] == base + i, fresh[b][t])
                    at = jnp.where(hit, b * 3 + t - 1, at)
                total.append(compact[at])
            out.append(total)
        return out

    order = ((1, 2), (1, 1), (1, 3), (0, 2), (1, 0), (0, 1), (0, 3), (0, 0))
    sib_at = {}
    for dz, dy in order:
        j = dz * 4 + dy
        for i, (p0, p1) in enumerate(pieces(dz, dy, 1)):
            to_sib[j, i * 128 : i * 128 + 128, :] = p0 + p1
        sib_at[j] = net.send(to_sib.at[j], from_sib.at[j], sib)

    def chip_sum(dz, dy, half):
        p0, p1 = pieces(dz, dy, 0)[half]
        j = dz * 4 + dy
        return (
            p0.astype(F32) + p1.astype(F32)
            + from_sib[j, half * 128 : half * 128 + 128, :].astype(F32)
        )

    def half_of(ref, half):
        return ref[half * 128 : half * 128 + 128, :].astype(F32)

    def outgoing(buf, dz, dy, extra=()):
        for half in range(2):
            total = chip_sum(dz, dy, half)
            for ref in extra:
                total = total + half_of(ref, half)
            buf[half * 128 : half * 128 + 128, :] = total.astype(BF16)

    def sib_landed(dz, dy):
        j = dz * 4 + dy
        net.landed(sib_at[j], from_sib.at[j])

    sib_landed(1, 2)
    outgoing(sum_z.at[0], 1, 2)
    s_z2 = net.send(sum_z.at[0], r_z2, zp)
    sib_landed(1, 1)
    outgoing(sum_y.at[0], 1, 1)
    s_ya = net.send(sum_y.at[0], r_ya, yp)
    sib_landed(1, 3)
    outgoing(sum_y.at[1], 1, 3)
    s_yb = net.send(sum_y.at[1], r_yb, ym)

    gp[:, G_V : G_V + 512] = dot_tn(normed[...], dv_all).astype(BF16)
    gp[:, G_K : G_K + 512] = dot_tn(normed[...], dk_all).astype(BF16)
    dq = jnp.concatenate([(grad_q[h] * q_slope[h]).astype(BF16) for h in range(4)], axis=1)
    gp[:, G_Q : G_Q + 512] = dot_tn(own_normed[...], dq).astype(BF16)
    own_grad[...] += dot_nt(dq, w[:, 1024:1536])

    half_cols = GCOLS // 2
    mine = pl.ds(pl.multiple_of(core * half_cols, half_cols), half_cols)
    other = pl.ds(pl.multiple_of((1 - core) * half_cols, half_cols), half_cols)
    s_g = net.send(gp.at[:, other], g_sib, sib)

    sib_landed(0, 2)
    net.landed(s_z2, r_z2)
    outgoing(sum_y.at[2], 0, 2, (r_z2,))
    s_h0 = net.send(sum_y.at[2, pl.ds(0, 128)], r_h.at[0], yp)
    s_h1 = net.send(sum_y.at[2, pl.ds(128, 128)], r_h.at[1], ym)

    net.landed(s_g, g_sib)
    for r in range(4):
        part = pl.ds(r * 128, 128)
        g_sib[part, :] = (gp[part, mine].astype(F32) + g_sib[part, :].astype(F32)).astype(BF16)

    def span(v, n):
        return pl.ds(pl.multiple_of(v * n, n), n)

    x_at = [
        net.send(g_sib.at[span(rot(x, i), 128)], g_x.at[i], ring_x[i]) for i in (1, 3, 2)
    ]

    sib_landed(1, 0)
    net.landed(s_ya, r_ya)
    net.landed(s_yb, r_yb)
    outgoing(sum_z.at[1], 1, 0, (r_ya, r_yb))
    s_z0 = net.send(sum_z.at[1], r_z0, zp)

    sib_landed(0, 1)
    sib_landed(0, 3)
    net.landed(s_h0, r_h.at[0])
    net.landed(s_h1, r_h.at[1])
    sum_y[3, 0:128, :] = (chip_sum(0, 1, 0) + r_h[0].astype(F32)).astype(BF16)
    sum_y[3, 128:256, :] = chip_sum(0, 1, 1).astype(BF16)
    s_p = net.send(sum_y.at[3], r_p, yp)
    sum_y[4, 0:128, :] = chip_sum(0, 3, 0).astype(BF16)
    sum_y[4, 128:256, :] = (chip_sum(0, 3, 1) + r_h[1].astype(F32)).astype(BF16)
    s_m = net.send(sum_y.at[4], r_m, ym)

    for at, i in zip(x_at, (1, 3, 2)):
        net.landed(at, g_x.at[i])
    g_x[0] = (
        g_sib[span(x, 128), :].astype(F32)
        + g_x[1].astype(F32) + g_x[2].astype(F32) + g_x[3].astype(F32)
    ).astype(BF16)
    z_at = [
        net.send(g_x.at[0, span(rot(z, i), 32)], g_z.at[i], ring_z[i]) for i in (1, 3, 2)
    ]

    sib_landed(0, 0)
    net.landed(s_p, r_p)
    net.landed(s_m, r_m)
    net.landed(s_z0, r_z0)
    for half in range(2):
        part = pl.ds(half * 128, 128)
        total = own_grad[part, :] + chip_sum(0, 0, half)
        for ref in (r_p, r_m, r_z0):
            total = total + half_of(ref, half)
        grad_events[part, :] = (
            upstream[part, :].astype(F32) + norm_back(total, hat_in[part, :], inv_in[part, :])
        ).astype(BF16)

    for at, i in zip(z_at, (1, 3, 2)):
        net.landed(at, g_z.at[i])
    g_zs[...] = (
        g_x[0, span(z, 32), :].astype(F32)
        + g_z[1].astype(F32) + g_z[2].astype(F32) + g_z[3].astype(F32)
    ).astype(BF16)
    g_y[y] = g_zs[...]
    y_at = [net.send(g_zs, g_y.at[y], ring_y[i]) for i in (1, 3, 2)]
    for at, i in zip(y_at, (3, 1, 2)):
        net.landed(at, g_y.at[rot(y, i)])
    final = (
        g_y[0].astype(F32) + g_y[1].astype(F32) + g_y[2].astype(F32) + g_y[3].astype(F32)
    ).astype(BF16)

    def block(vx, vz=None):
        if vz is None:
            return pl.ds(pl.multiple_of(vx * 128, 128), 128)
        return pl.ds(pl.multiple_of(vx * 128 + vz * 32, 32), 32)

    gw[block(x, z), mine] = final
    here = gw.at[block(x, z), mine]
    z_at = [net.send(here, here, ring_z[i]) for i in (1, 3, 2)]
    for at, i in zip(z_at, (3, 1, 2)):
        net.landed(at, gw.at[block(x, rot(z, i)), mine])
    here = gw.at[block(x), mine]
    x_at = [net.send(here, here, ring_x[i]) for i in (1, 3, 2)]
    sib_back = [net.send(here, here, sib)]
    for at, i in zip(x_at, (3, 1, 2)):
        there = gw.at[block(rot(x, i)), mine]
        net.landed(at, there)
        sib_back.append(net.send(there, there, sib))
    for at, i in zip(sib_back, (0, 3, 1, 2)):
        net.landed(at, gw.at[block(rot(x, i)), other])
    net.drain()


def local(events, upstream, lengths, block_slots, pattern, in_weight, out_weight):
    vmem = pl.BlockSpec(memory_space=pltpu.VMEM)
    smem = pl.BlockSpec(memory_space=pltpu.SMEM)
    hbm = pl.BlockSpec(memory_space=pl.ANY)
    v = pltpu.VMEM
    half = GCOLS // 2
    scratch = [
        v((512, 2048), BF16), v((512, 512), BF16), v((32, 128, 512), BF16),
        v((1024, 512), BF16), v((256, 512), BF16), v((256, 512), F32), v((256, 1), F32),
        v((4, 256, 128), BF16), v((4, 256, 128), F32),
        v((4, 256, 128), BF16), v((4, 256, 128), F32),
        v((4, 1024, 128), BF16), v((4, 1024, 128), F32),
        v((4, 1024, 128), BF16), v((4, 1024, 128), F32),
        v((4, 256, 128), F32), v((2, 128, 512), F32), v((8, 128, 512), BF16),
        v((8, 128, 512), F32), v((4, 256, 128), F32), v((4, 256, 128), BF16),
        v((4, 256, 128), F32),
        v((4, 1024, 128), BF16), v((4, 1024, 128), BF16), v((256, 512), F32),
        v((7, 128, 512), BF16),
        v((8, 256, 512), BF16), v((8, 256, 512), BF16), v((5, 256, 512), BF16),
        v((2, 256, 512), BF16),
        v((256, 512), BF16), v((256, 512), BF16), v((256, 512), BF16), v((2, 128, 512), BF16),
        v((256, 512), BF16), v((256, 512), BF16), v((256, 512), BF16),
        v((512, GCOLS), BF16), v((512, half), BF16), v((4, 128, half), BF16), v((4, 32, half), BF16),
        v((4, 32, half), BF16), v((32, half), BF16),
        pltpu.SemaphoreType.DMA((2,)),
        pltpu.SemaphoreType.DMA((N_SEM,)),
        pltpu.SemaphoreType.DMA((N_SEM,)),
    ]
    encoded, grad_events, gw = pl.pallas_call(
        layer_kernel,
        out_shape=(
            jax.ShapeDtypeStruct((256, D), BF16),
            jax.ShapeDtypeStruct((256, D), BF16),
            jax.ShapeDtypeStruct((512, GCOLS), BF16),
        ),
        in_specs=[smem, smem, smem, vmem, vmem, hbm, hbm],
        out_specs=(vmem, vmem, vmem),
        scratch_shapes=scratch,
        compiler_params=pltpu.CompilerParams(
            collective_id=0, has_side_effects=True, vmem_limit_bytes=56 * 2**20
        ),
        name="layer",
    )(block_slots, pattern, lengths, events[0], upstream[0], in_weight, out_weight)
    grad_in = jnp.concatenate(
        [gw[:, g : g + 512] for g in (G_U, G_V, G_Q, G_K)], axis=1
    ).astype(F32)
    grad_out = gw[:, G_OUT : G_OUT + 512].astype(F32)
    return encoded[None], grad_events[None], grad_in, grad_out


def solution(mesh):
    return jax.shard_map(
        local,
        mesh=mesh,
        in_specs=(P("dp", "ctx", None), P("dp", "ctx", None), P("dp"), P(), P(), P(), P()),
        out_specs=(P("dp", "ctx", None), P("dp", "ctx", None), P(), P()),
        check_vma=False,
    )
```

time: 432 us -> 105 us (0.24)
  waiting for transfers between devices: 302 us -> 0 us
  Pallas kernels: 0 us -> 94.8 us
  local copies, waits for them, and re-layouts: 50.9 us -> 2.78 us
  other arithmetic: 35.1 us -> 5.53 us
  matrix products: 28 us -> 0 us
  between operations: 14.7 us -> 1.29 us
    psum x1 -> x0, waiting for transfers between devices: 154 us -> none  [local(): grad_in, grad_out = lax.psum((grad_in, grad_out), ('dp', 'ctx'))]
    reduce_scatter x2 -> x0, waiting for transfers between devices: 97.1 us -> none  [the longest x1 65.9 us: local(): lax.psum_scatter(spread_v.astype(jnp.bfloat16), 'ctx', scatter_dimension=...]
    pallas_call x0 -> x1, Pallas kernels: none -> 94.8 us  [local(): pl.pallas_call(layer_kernel, out_shape=(jax.ShapeDtypeStruct((256, D), BF...]
    all_gather x1 -> x0, waiting for transfers between devices: 51.5 us -> none  [local(): whole = lax.all_gather(source, 'ctx', axis=0, tiled=True)]
    dot_general x12 -> x0, matrix products: 28 us -> none  [the longest x1 3.4 us: local(): jnp.einsum('bihd,bjhd->bhij', q_blk, k_sel, preferred_element_type=f32)]
    reshape x8 -> x0, local copies, waits for them, and re-layouts: 13.1 us -> none  [the longest x2 4.54 us: local(): k_sel = picked[:, :width].reshape(per_dev, KEYS, HEADS, HD)]
    convert_element_type x6 -> x2, other arithmetic: 17.8 us -> 5.53 us  [the longest x1 2.97 us: local(): grad_out = gw[:, G_OUT:G_OUT + 512].astype(F32)]
    scatter-add x2 -> x0, other arithmetic: 10.3 us -> none  [the longest x1 5.15 us: local(): jnp.zeros((blocks, BLK, width), f32).at[index].add(grad_v_sel)]
  transfers between devices with their start and end apart: 4 -> 0, of which waited for: 4 -> 0; matrix products, arithmetic and copies ran while one was open for 10% -> 0% of each run, Pallas kernels for 0% -> 0%
where the time goes in v1:
time: 105 us; the launch traced here: 104 us
  Pallas kernels  94.8 us (90%)
  other arithmetic  5.53 us (5%)
  local copies, waits for them, and re-layouts  2.78 us (3%)
  between operations  1.29 us (1%)
    pallas_call x1, Pallas kernels, local(): pl.pallas_call(layer_kernel, out_shape=(jax.ShapeDtypeStruct((256, D), BF...  94.8 us
    convert_element_type x1, other arithmetic, local(): grad_out = gw[:, G_OUT:G_OUT + 512].astype(F32)  2.97 us
    unnamed x7, local copies, waits for them, and re-layouts  2.78 us
    convert_element_type x1, other arithmetic, local(): grad_in = jnp.concatenate([gw[:, g:g + 512] for g in (G_U, G_V, G_Q, G_K)...  2.56 us

profile of v1, /device:TPU:1, one launch (start us, length us, event | category | flops | bytes accessed | tf_op | source)
XLA Modules:
  0.0 104.4 jit_solution(9021797455091814945)
XLA Ops:
  1.3 1.4 %copy.11.pattern_ref = s32[32,3]{1,0:T(8,128)} copy(s32[32,3]{0,1:T(4,128)} %param.11) | data formatting | bytes 768 | tf_op args[4]
  2.6 94.8 %layer.1 = (bf16[256,512]{1,0:T(8,128)(2,1)}, bf16[256,512]{1,0:T(8,128)(2,1)}, bf16[512,2560]{1,0:T(8,128)(2,1)}) custom-call(s32[32]{0:T(128)} %slots_ref.1, s32[32,3]{1,0:T(8,128)} %copy.11.pattern_ref, s32[1]{0:T(128)S(6)} %copy.14.length_ref, bf16[256,512]{1,0:T(8,128)(2,1)} %bitcast.4, bf16[256,512]{1,0:T(8,128)(2,1)} %bitcast.5, ...), custom_call_target="tpu_custom_call" | custom-call | tf_op jit(solution)/shard_map/layer/pallas_call | solution.py:523
  97.5 3.0 %slice_convert_fusion = (f32[512,512]{1,0:T(8,128)}, bf16[512,512]{1,0:T(8,128)(2,1)S(1)}, bf16[512,512]{1,0:T(8,128)(2,1)S(1)}, bf16[512,512]{1,0:T(8,128)(2,1)S(1)}, bf16[512,512]{1,0:T(8,128)(2,1)S(1)}) fusion(bf16[512,2560]{1,0:T(8,128)(2,1)} %get-tuple-element.9), kind=kLoop, calls=%fused_computation.1 | loop fusion | flops 262144 | bytes 5767168 | tf_op jit(solution)/shard_map/convert_element_type | solution.py:541
  100.4 0.0 copy-start.1
  100.4 0.0 copy-start
  100.4 2.6 %maximum_convert_fusion = f32[512,2048]{1,0:T(8,128)} fusion(bf16[512,512]{1,0:T(8,128)(2,1)S(1)} %get-tuple-element.11, bf16[512,512]{1,0:T(8,128)(2,1)S(1)} %get-tuple-element.12, bf16[512,512]{1,0:T(8,128)(2,1)S(1)} %get-tuple-element.13, bf16[512,512]{1,0:T(8,128)(2,1)S(1)} %get-tuple-element.14), kind=kLoop, calls=%fused_computation | loop fusion | flops 8388608 | bytes 6291456 | tf_op jit(solution)/shard_map/convert_element_type | solution.py:540
  103.0 0.0 copy-done.1
  103.0 0.7 copy.15
  103.7 0.0 copy-done
  103.7 0.7 copy.16
Async XLA Ops:
  100.4 2.6 %copy-start.1 = (bf16[256,512]{1,0:T(8,128)(2,1)S(1)}, bf16[256,512]{1,0:T(8,128)(2,1)}, u32[]{:S(2)}) copy-start(bf16[256,512]{1,0:T(8,128)(2,1)} %get-tuple-element.7) | copy-start | bytes 786436
  100.4 3.3 %copy-start = (bf16[256,512]{1,0:T(8,128)(2,1)S(1)}, bf16[256,512]{1,0:T(8,128)(2,1)}, u32[]{:S(2)}) copy-start(bf16[256,512]{1,0:T(8,128)(2,1)} %get-tuple-element.8) | copy-start | bytes 786436

commit v2 on v1

--- a/solution.py
+++ b/solution.py
@@ -17,9 +17,23 @@
 F32 = jnp.float32
 BF16 = jnp.bfloat16
 FAR = 1 << 20
-G_OUT, G_U, G_Q, G_V, G_K = 0, 512, 1024, 1536, 2048
+G_OUT, G_U, G_V, G_Q, G_K = 0, 512, 1024, 1536, 2048
 GCOLS = 2560
-N_SEM = 96
+N_SEM = 176
+PARTS = (
+    ("ou", G_OUT, 1024, ("y", "x", "z")),
+    ("v", G_V, 512, ("x", "z", "y")),
+    ("k", G_K, 512, ("x", "y", "z")),
+    ("q", G_Q, 512, ("z", "x", "y")),
+)
+SCHEDULE = (
+    "ou", "value_heads", "score_heads", "ou", "weight_k", "weight_q", "weight_v", "v", "q",
+    "k", "back_rows", "d2d_a", "q", "k", "v", "far_z", "far_y", "d2d_b",
+    "ou", "q", "k", "own_rows", "encode", "near_free", "last_own", "v", "ou",
+    "halves", "q", "v", "k", "near_z", "ou", "k", "ou", "q",
+    "near_tied", "v", "k", "q", "v", "k", "ou", "q", "k",
+    "v", "ou", "last", "q", "v",
+)
 
 
 def dot(a, b):
@@ -92,11 +106,11 @@
     w, wo, gx, normed, own_normed, hat_in, inv_in,
     u_act, u_slope, q_act, q_slope, k_act, k_slope, v_act, v_slope,
     grad_gated, limit_mask, weights, slope, mixed, grad_mixed, grad_q,
-    dv, dk, own_grad, compact,
+    gated, du, dq, dv, dk, own_grad, compact,
     to_sib, from_sib, sum_y, sum_z, r_z2, r_ya, r_yb, r_h, r_p, r_m, r_z0,
-    gp, g_sib, g_x, g_z, g_y, g_zs,
-    w_sems, send_sems, recv_sems,
+    gp, gf, *rest,
 ):
+    ar_bufs, (ar_sems, w_sems, send_sems, recv_sems) = tuple(rest[:-4]), rest[-4:]
     dp = lax.axis_index("dp")
     ctx = lax.axis_index("ctx")
     x, zh = dp // 2, dp % 2
@@ -217,7 +231,7 @@
     listed, at_slot, fresh = [], [], []
     for b in range(2):
         mine = slots_ref[2 * ctx + b]
-        picks = [mine] + [pattern_ref[mine, t] for t in range(3)]
+        picks = [mine] + [pattern_ref[t, mine] for t in range(3)]
         listed.append(picks)
         news = [None]
         for t in range(1, 4):
@@ -283,7 +297,7 @@
         )
         return carry
 
-    lax.fori_loop(0, 8, forward_head, 0)
+    lax.fori_loop(0, 8, forward_head, 0, unroll=8)
 
     def across(parts):
         return sum(jnp.sum(part, axis=-1, keepdims=True) for part in parts) * (1.0 / D)
@@ -294,20 +308,113 @@
     inv_mix = lax.rsqrt(across([part * part for part in parts]) + EPS)
     hats = [part * inv_mix for part in parts]
     us = [u_act[h].astype(F32) for h in range(4)]
-    gated = jnp.concatenate([(hats[h] * us[h]).astype(BF16) for h in range(4)], axis=1)
-    encoded[...] = (events[...].astype(F32) + dot(gated, wo[...])).astype(BF16)
-    gp[:, G_OUT : G_OUT + 512] = dot_tn(gated, upstream[...]).astype(BF16)
+    gated[...] = jnp.concatenate([(hats[h] * us[h]).astype(BF16) for h in range(4)], axis=1)
     ggs = [grad_gated[h] for h in range(4)]
-    du = jnp.concatenate([(ggs[h] * hats[h] * u_slope[h]).astype(BF16) for h in range(4)], axis=1)
-    gp[:, G_U : G_U + 512] = dot_tn(own_normed[...], du).astype(BF16)
-    own_grad[...] = dot_nt(du, w[:, 0:512])
+    du[...] = jnp.concatenate(
+        [(ggs[h] * hats[h] * u_slope[h]).astype(BF16) for h in range(4)], axis=1
+    )
     ts = [ggs[h] * us[h] for h in range(4)]
     mean_t = across(ts)
     mean_th = across([ts[h] * hats[h] for h in range(4)])
     for h in range(4):
         grad_mixed[h] = (inv_mix * (ts[h] - mean_t - hats[h] * mean_th)).astype(BF16)
-
-    def backward_head(i, carry):
+    gp[:, G_OUT : G_OUT + 512] = dot_tn(gated[...], upstream[...]).astype(BF16)
+    gp[:, G_U : G_U + 512] = dot_tn(own_normed[...], du[...]).astype(BF16)
+
+    place = {"x": x, "y": y, "z": z}
+    rings = {"x": ring_x, "y": ring_y, "z": ring_z}
+
+    def span(start, n):
+        return pl.ds(pl.multiple_of(start, n), n)
+
+    def add4(parts):
+        return sum(part.astype(F32) for part in parts).astype(BF16)
+
+    def reduce_columns(lo, n, axes, bufs):
+        sibling, first, second, third, total, local_sem = bufs
+        a1, a2, a3 = axes
+        p1, p2, p3 = (place[a] for a in axes)
+        half = n // 2
+        mine = pl.ds(pl.multiple_of(lo + core * half, 128), half)
+        other = pl.ds(pl.multiple_of(lo + (1 - core) * half, 128), half)
+        far_first, near_first = (1, 3, 2), (3, 1, 2)
+
+        def rows1(p):
+            return span(p * 128, 128)
+
+        def rows2(p):
+            return span(p1 * 128 + p * 32, 32)
+
+        at = net.send(gp.at[:, other], sibling, sib)
+        yield
+        net.landed(at, sibling)
+        ats = []
+        for i in far_first + (0,):
+            block = rows1(rot(p1, i))
+            sibling[block, :] = gp[block, mine] + sibling[block, :]
+            if i:
+                ats.append(net.send(sibling.at[block], first.at[i], rings[a1][i]))
+        yield
+        for at, i in zip(ats, far_first):
+            net.landed(at, first.at[i])
+        first[0] = add4([sibling[rows1(p1), :], first[1], first[2], first[3]])
+        ats = [
+            net.send(first.at[0, span(rot(p2, i) * 32, 32)], second.at[i], rings[a2][i])
+            for i in far_first
+        ]
+        yield
+        for at, i in zip(ats, far_first):
+            net.landed(at, second.at[i])
+        total[...] = add4([first[0, span(p2 * 32, 32), :], second[1], second[2], second[3]])
+        third[p3] = total[...]
+        ats = [net.send(total, third.at[p3], rings[a3][i]) for i in far_first]
+        yield
+        for at, i in zip(ats, near_first):
+            net.landed(at, third.at[rot(p3, i)])
+        gf[rows2(p2), mine] = add4([third[0], third[1], third[2], third[3]])
+        here = gf.at[rows2(p2), mine]
+        ats = [net.send(here, here, rings[a2][i]) for i in far_first]
+        yield
+        for at, i in zip(ats, near_first):
+            net.landed(at, gf.at[rows2(rot(p2, i)), mine])
+        here, there = gf.at[rows1(p1), mine], gw.at[rows1(p1), mine]
+        ats = [net.send(here, there, rings[a1][i]) for i in far_first]
+        back = [net.send(here, there, sib)]
+        keep = pltpu.make_async_copy(here, there, local_sem)
+        keep.start()
+        yield
+        for at, i in zip(ats, near_first):
+            there = gw.at[rows1(rot(p1, i)), mine]
+            net.landed(at, there)
+            back.append(net.send(there, there, sib))
+        yield
+        for at, i in zip(back, (0,) + near_first):
+            net.landed(at, gw.at[rows1(rot(p1, i)), other])
+        keep.wait()
+        yield
+
+    parts = {
+        name: reduce_columns(lo, n, axes, ar_bufs[5 * i : 5 * i + 5] + (ar_sems.at[i],))
+        for i, (name, lo, n, axes) in enumerate(PARTS)
+    }
+
+    def heads_of(ref):
+        return jnp.concatenate([ref[h] for h in range(4)], axis=1)
+
+    def value_head(i, carry):
+        b, h = i // 4, i % 4
+        k_rows = pl.ds(pl.multiple_of(b * 512, 512), 512)
+        gm = grad_mixed[h, pl.ds(pl.multiple_of(b * 128, 128), 128), :]
+        dv[h, k_rows, :] = (dot_tn(weights[i], gm) * v_slope[h, k_rows, :]).astype(BF16)
+        return carry
+
+    def value_heads():
+        lax.fori_loop(0, 8, value_head, 0, unroll=8)
+
+    def weight_v():
+        gp[:, G_V : G_V + 512] = dot_tn(normed[...], heads_of(dv)).astype(BF16)
+
+    def score_head(i, carry):
         b, h = i // 4, i % 4
         q_rows = pl.ds(pl.multiple_of(b * 128, 128), 128)
         k_rows = pl.ds(pl.multiple_of(b * 512, 512), 512)
@@ -316,180 +423,190 @@
         gs = (dot_nt(gm, v_act[h, k_rows, :]) * slope[i]).astype(BF16)
         grad_q[h, q_rows, :] = dot(gs, k_act[h, k_rows, :])
         dk[h, k_rows, :] = (dot_tn(gs, q) * k_slope[h, k_rows, :]).astype(BF16)
-        dv[h, k_rows, :] = (dot_tn(weights[i], gm) * v_slope[h, k_rows, :]).astype(BF16)
         return carry
 
-    lax.fori_loop(0, 8, backward_head, 0)
-
-    dv_all = jnp.concatenate([dv[h] for h in range(4)], axis=1)
-    dk_all = jnp.concatenate([dk[h] for h in range(4)], axis=1)
-    back = dot_nt(dv_all, w[:, 512:1024]) + dot_nt(dk_all, w[:, 1536:2048])
-    for b in range(2):
-        for t in range(1, 4):
-            lo = b * 512 + t * 128
-            compact[b * 3 + t - 1] = back[lo : lo + 128].astype(BF16)
-        own_grad[b * 128 : b * 128 + 128, :] += back[b * 512 : b * 512 + 128]
-    compact[6] = jnp.zeros((128, 512), BF16)
-
-    def pieces(dz, dy, side):
+    def score_heads():
+        lax.fori_loop(0, 8, score_head, 0, unroll=8)
+
+    def weight_k():
+        gp[:, G_K : G_K + 512] = dot_tn(normed[...], heads_of(dk)).astype(BF16)
+
+    def weight_q():
+        dq[...] = jnp.concatenate(
+            [(grad_q[h] * q_slope[h]).astype(BF16) for h in range(4)], axis=1
+        )
+        gp[:, G_Q : G_Q + 512] = dot_tn(own_normed[...], dq[...]).astype(BF16)
+
+    def back_rows():
+        back = dot_nt(heads_of(dv), w[:, 512:1024]) + dot_nt(heads_of(dk), w[:, 1536:2048])
+        for b in range(2):
+            for t in range(1, 4):
+                lo = b * 512 + t * 128
+                compact[b * 3 + t - 1] = back[lo : lo + 128].astype(BF16)
+            own_grad[b * 128 : b * 128 + 128, :] = back[b * 512 : b * 512 + 128]
+        compact[6] = jnp.zeros((128, 512), BF16)
+
+    def encode():
+        encoded[...] = (events[...].astype(F32) + dot(gated[...], wo[...])).astype(BF16)
+
+    def own_rows():
+        own_grad[...] += dot_nt(du[...], w[:, 0:512]) + dot_nt(dq[...], w[:, 1024:1536])
+
+    def piece(dz, dy, side, half):
         zz = zl if dz == 0 else 1 - zl
         kk = core if side == 0 else 1 - core
-        base = ((zz * 4 + rot(y, dy)) * 2 + kk) * 2
-        out = []
-        for i in range(2):
-            total = []
-            for b in range(2):
-                at = jnp.int32(6)
-                for t in range(1, 4):
-                    hit = jnp.logical_and(found[b][t] == base + i, fresh[b][t])
-                    at = jnp.where(hit, b * 3 + t - 1, at)
-                total.append(compact[at])
-            out.append(total)
-        return out
-
-    order = ((1, 2), (1, 1), (1, 3), (0, 2), (1, 0), (0, 1), (0, 3), (0, 0))
-    sib_at = {}
-    for dz, dy in order:
+        slot = ((zz * 4 + rot(y, dy)) * 2 + kk) * 2 + half
+        both = []
+        for b in range(2):
+            at = jnp.int32(6)
+            for t in range(1, 4):
+                hit = jnp.logical_and(found[b][t] == slot, fresh[b][t])
+                at = jnp.where(hit, b * 3 + t - 1, at)
+            both.append(compact[at])
+        return both[0] + both[1]
+
+    HALF = (pl.ds(0, 128), pl.ds(128, 128))
+    sib_at, sib_here, sent = {}, set(), {}
+
+    def to_sibling(order):
+        for dz, dy in order:
+            j = dz * 4 + dy
+            for half in range(2):
+                to_sib[j, HALF[half], :] = piece(dz, dy, 1, half)
+            sib_at[j] = net.send(to_sib.at[j], from_sib.at[j], sib)
+
+    def chip_sum(dz, dy, half):
         j = dz * 4 + dy
-        for i, (p0, p1) in enumerate(pieces(dz, dy, 1)):
-            to_sib[j, i * 128 : i * 128 + 128, :] = p0 + p1
-        sib_at[j] = net.send(to_sib.at[j], from_sib.at[j], sib)
-
-    def chip_sum(dz, dy, half):
-        p0, p1 = pieces(dz, dy, 0)[half]
-        j = dz * 4 + dy
-        return (
-            p0.astype(F32) + p1.astype(F32)
-            + from_sib[j, half * 128 : half * 128 + 128, :].astype(F32)
-        )
-
-    def half_of(ref, half):
-        return ref[half * 128 : half * 128 + 128, :].astype(F32)
-
-    def outgoing(buf, dz, dy, extra=()):
+        if j not in sib_here:
+            net.landed(sib_at[j], from_sib.at[j])
+            sib_here.add(j)
+        return piece(dz, dy, 0, half) + from_sib[j, HALF[half], :]
+
+    def pass_on(name, buf, dz, dy, half, there, device, extra=()):
+        total = chip_sum(dz, dy, half)
+        for other_name, ref in extra:
+            net.landed(sent[other_name, half], ref)
+            total = total + ref[...]
+        buf[HALF[half], :] = total
+        sent[name, half] = net.send(buf.at[HALF[half]], there, device)
+
+    def d2d_a():
+        to_sibling(((1, 2), (1, 1), (1, 3)))
+
+    def d2d_b():
+        to_sibling(((0, 2), (1, 0), (0, 1), (0, 3), (0, 0)))
+
+    def far_z():
         for half in range(2):
-            total = chip_sum(dz, dy, half)
-            for ref in extra:
-                total = total + half_of(ref, half)
-            buf[half * 128 : half * 128 + 128, :] = total.astype(BF16)
-
-    def sib_landed(dz, dy):
-        j = dz * 4 + dy
-        net.landed(sib_at[j], from_sib.at[j])
-
-    sib_landed(1, 2)
-    outgoing(sum_z.at[0], 1, 2)
-    s_z2 = net.send(sum_z.at[0], r_z2, zp)
-    sib_landed(1, 1)
-    outgoing(sum_y.at[0], 1, 1)
-    s_ya = net.send(sum_y.at[0], r_ya, yp)
-    sib_landed(1, 3)
-    outgoing(sum_y.at[1], 1, 3)
-    s_yb = net.send(sum_y.at[1], r_yb, ym)
-
-    gp[:, G_V : G_V + 512] = dot_tn(normed[...], dv_all).astype(BF16)
-    gp[:, G_K : G_K + 512] = dot_tn(normed[...], dk_all).astype(BF16)
-    dq = jnp.concatenate([(grad_q[h] * q_slope[h]).astype(BF16) for h in range(4)], axis=1)
-    gp[:, G_Q : G_Q + 512] = dot_tn(own_normed[...], dq).astype(BF16)
-    own_grad[...] += dot_nt(dq, w[:, 1024:1536])
-
-    half_cols = GCOLS // 2
-    mine = pl.ds(pl.multiple_of(core * half_cols, half_cols), half_cols)
-    other = pl.ds(pl.multiple_of((1 - core) * half_cols, half_cols), half_cols)
-    s_g = net.send(gp.at[:, other], g_sib, sib)
-
-    sib_landed(0, 2)
-    net.landed(s_z2, r_z2)
-    outgoing(sum_y.at[2], 0, 2, (r_z2,))
-    s_h0 = net.send(sum_y.at[2, pl.ds(0, 128)], r_h.at[0], yp)
-    s_h1 = net.send(sum_y.at[2, pl.ds(128, 128)], r_h.at[1], ym)
-
-    net.landed(s_g, g_sib)
-    for r in range(4):
-        part = pl.ds(r * 128, 128)
-        g_sib[part, :] = (gp[part, mine].astype(F32) + g_sib[part, :].astype(F32)).astype(BF16)
-
-    def span(v, n):
-        return pl.ds(pl.multiple_of(v * n, n), n)
-
-    x_at = [
-        net.send(g_sib.at[span(rot(x, i), 128)], g_x.at[i], ring_x[i]) for i in (1, 3, 2)
+            pass_on("z2", sum_z.at[0], 1, 2, half, r_z2.at[HALF[half]], zp)
+
+    def far_y():
+        for half in range(2):
+            pass_on("ya", sum_y.at[0], 1, 1, half, r_ya.at[HALF[half]], yp)
+            pass_on("yb", sum_y.at[1], 1, 3, half, r_yb.at[HALF[half]], ym)
+
+    def near_free():
+        pass_on("p", sum_y.at[3], 0, 1, 1, r_p.at[HALF[1]], yp)
+        pass_on("m", sum_y.at[4], 0, 3, 0, r_m.at[HALF[0]], ym)
+
+    def halves():
+        for half in range(2):
+            pass_on(
+                "h", sum_y.at[2], 0, 2, half, r_h.at[half], (yp, ym)[half],
+                (("z2", r_z2.at[HALF[half]]),),
+            )
+
+    def near_z():
+        for half in range(2):
+            pass_on(
+                "z0", sum_z.at[1], 1, 0, half, r_z0.at[HALF[half]], zp,
+                (("ya", r_ya.at[HALF[half]]), ("yb", r_yb.at[HALF[half]])),
+            )
+
+    def near_tied():
+        pass_on("p", sum_y.at[3], 0, 1, 0, r_p.at[HALF[0]], yp, (("h", r_h.at[0]),))
+        pass_on("m", sum_y.at[4], 0, 3, 1, r_m.at[HALF[1]], ym, (("h", r_h.at[1]),))
+
+    def last_own():
+        for half in range(2):
+            own_grad[HALF[half], :] += chip_sum(0, 0, half).astype(F32)
+
+    def last():
+        for half in range(2):
+            total = own_grad[HALF[half], :]
+            for name, ref in (("p", r_p), ("m", r_m), ("z0", r_z0)):
+                net.landed(sent[name, half], ref.at[HALF[half]])
+                total = total + ref[HALF[half], :].astype(F32)
+            grad_events[HALF[half], :] = (
+                upstream[HALF[half], :].astype(F32)
+                + norm_back(total, hat_in[HALF[half], :], inv_in[HALF[half], :])
+            ).astype(BF16)
+
+    steps = dict(
+        value_heads=value_heads, weight_v=weight_v, score_heads=score_heads, weight_k=weight_k,
+        weight_q=weight_q, back_rows=back_rows, encode=encode, own_rows=own_rows, d2d_a=d2d_a,
+        d2d_b=d2d_b, far_z=far_z, far_y=far_y, near_free=near_free, halves=halves,
+        near_z=near_z, near_tied=near_tied, last_own=last_own, last=last,
+    )
+    for step in SCHEDULE:
+        if step in parts:
+            next(parts[step])
+        else:
+            steps[step]()
+    net.drain()
+
+
+def finish_kernel(
+    gw, enc, gev, grad_in, grad_out, encoded, grad_events, got, full, rest, in_sems, out_sems
+):
+    rows = [pl.ds(i * 128, 128) for i in range(4)]
+    reads = [pltpu.make_async_copy(gw.at[r], got.at[r], in_sems.at[i]) for i, r in enumerate(rows)]
+    reads += [
+        pltpu.make_async_copy(enc, rest.at[0], in_sems.at[4]),
+        pltpu.make_async_copy(gev, rest.at[1], in_sems.at[5]),
     ]
-
-    sib_landed(1, 0)
-    net.landed(s_ya, r_ya)
-    net.landed(s_yb, r_yb)
-    outgoing(sum_z.at[1], 1, 0, (r_ya, r_yb))
-    s_z0 = net.send(sum_z.at[1], r_z0, zp)
-
-    sib_landed(0, 1)
-    sib_landed(0, 3)
-    net.landed(s_h0, r_h.at[0])
-    net.landed(s_h1, r_h.at[1])
-    sum_y[3, 0:128, :] = (chip_sum(0, 1, 0) + r_h[0].astype(F32)).astype(BF16)
-    sum_y[3, 128:256, :] = chip_sum(0, 1, 1).astype(BF16)
-    s_p = net.send(sum_y.at[3], r_p, yp)
-    sum_y[4, 0:128, :] = chip_sum(0, 3, 0).astype(BF16)
-    sum_y[4, 128:256, :] = (chip_sum(0, 3, 1) + r_h[1].astype(F32)).astype(BF16)
-    s_m = net.send(sum_y.at[4], r_m, ym)
-
-    for at, i in zip(x_at, (1, 3, 2)):
-        net.landed(at, g_x.at[i])
-    g_x[0] = (
-        g_sib[span(x, 128), :].astype(F32)
-        + g_x[1].astype(F32) + g_x[2].astype(F32) + g_x[3].astype(F32)
-    ).astype(BF16)
-    z_at = [
-        net.send(g_x.at[0, span(rot(z, i), 32)], g_z.at[i], ring_z[i]) for i in (1, 3, 2)
-    ]
-
-    sib_landed(0, 0)
-    net.landed(s_p, r_p)
-    net.landed(s_m, r_m)
-    net.landed(s_z0, r_z0)
-    for half in range(2):
-        part = pl.ds(half * 128, 128)
-        total = own_grad[part, :] + chip_sum(0, 0, half)
-        for ref in (r_p, r_m, r_z0):
-            total = total + half_of(ref, half)
-        grad_events[part, :] = (
-            upstream[part, :].astype(F32) + norm_back(total, hat_in[part, :], inv_in[part, :])
-        ).astype(BF16)
-
-    for at, i in zip(z_at, (1, 3, 2)):
-        net.landed(at, g_z.at[i])
-    g_zs[...] = (
-        g_x[0, span(z, 32), :].astype(F32)
-        + g_z[1].astype(F32) + g_z[2].astype(F32) + g_z[3].astype(F32)
-    ).astype(BF16)
-    g_y[y] = g_zs[...]
-    y_at = [net.send(g_zs, g_y.at[y], ring_y[i]) for i in (1, 3, 2)]
-    for at, i in zip(y_at, (3, 1, 2)):
-        net.landed(at, g_y.at[rot(y, i)])
-    final = (
-        g_y[0].astype(F32) + g_y[1].astype(F32) + g_y[2].astype(F32) + g_y[3].astype(F32)
-    ).astype(BF16)
-
-    def block(vx, vz=None):
-        if vz is None:
-            return pl.ds(pl.multiple_of(vx * 128, 128), 128)
-        return pl.ds(pl.multiple_of(vx * 128 + vz * 32, 32), 32)
-
-    gw[block(x, z), mine] = final
-    here = gw.at[block(x, z), mine]
-    z_at = [net.send(here, here, ring_z[i]) for i in (1, 3, 2)]
-    for at, i in zip(z_at, (3, 1, 2)):
-        net.landed(at, gw.at[block(x, rot(z, i)), mine])
-    here = gw.at[block(x), mine]
-    x_at = [net.send(here, here, ring_x[i]) for i in (1, 3, 2)]
-    sib_back = [net.send(here, here, sib)]
-    for at, i in zip(x_at, (3, 1, 2)):
-        there = gw.at[block(rot(x, i)), mine]
-        net.landed(at, there)
-        sib_back.append(net.send(there, there, sib))
-    for at, i in zip(sib_back, (0, 3, 1, 2)):
-        net.landed(at, gw.at[block(rot(x, i)), other])
-    net.drain()
+    for copy in reads:
+        copy.start()
+    writes = []
+    for i, r in enumerate(rows):
+        reads[i].wait()
+        full[r, :] = got[r, :].astype(F32)
+        writes += [
+            pltpu.make_async_copy(full.at[r, pl.ds(512, 2048)], grad_in.at[r], out_sems.at[i]),
+            pltpu.make_async_copy(full.at[r, pl.ds(0, 512)], grad_out.at[r], out_sems.at[4 + i]),
+        ]
+        for copy in writes[-2:]:
+            copy.start()
+    for i, (copy, out) in enumerate(zip(reads[4:], (encoded, grad_events))):
+        copy.wait()
+        writes.append(pltpu.make_async_copy(rest.at[i], out, out_sems.at[8 + i]))
+        writes[-1].start()
+    for copy in writes:
+        copy.wait()
+
+
+def finish(gw, enc, gev):
+    hbm = pl.BlockSpec(memory_space=pl.ANY)
+    return pl.pallas_call(
+        finish_kernel,
+        out_shape=(
+            jax.ShapeDtypeStruct((512, 2048), F32),
+            jax.ShapeDtypeStruct((512, 512), F32),
+            jax.ShapeDtypeStruct((256, D), BF16),
+            jax.ShapeDtypeStruct((256, D), BF16),
+        ),
+        in_specs=[hbm] * 3,
+        out_specs=(hbm,) * 4,
+        scratch_shapes=[
+            pltpu.VMEM((512, GCOLS), BF16),
+            pltpu.VMEM((512, GCOLS), F32),
+            pltpu.VMEM((2, 256, D), BF16),
+            pltpu.SemaphoreType.DMA((6,)),
+            pltpu.SemaphoreType.DMA((10,)),
+        ],
+        compiler_params=pltpu.CompilerParams(vmem_limit_bytes=60 * 2**20),
+        name="finish",
+    )(gw, enc, gev)
 
 
 def local(events, upstream, lengths, block_slots, pattern, in_weight, out_weight):
@@ -497,7 +614,6 @@
     smem = pl.BlockSpec(memory_space=pltpu.SMEM)
     hbm = pl.BlockSpec(memory_space=pl.ANY)
     v = pltpu.VMEM
-    half = GCOLS // 2
     scratch = [
         v((512, 2048), BF16), v((512, 512), BF16), v((32, 128, 512), BF16),
         v((1024, 512), BF16), v((256, 512), BF16), v((256, 512), F32), v((256, 1), F32),
@@ -508,14 +624,23 @@
         v((4, 256, 128), F32), v((2, 128, 512), F32), v((8, 128, 512), BF16),
         v((8, 128, 512), F32), v((4, 256, 128), F32), v((4, 256, 128), BF16),
         v((4, 256, 128), F32),
+        v((256, 512), BF16), v((256, 512), BF16), v((256, 512), BF16),
         v((4, 1024, 128), BF16), v((4, 1024, 128), BF16), v((256, 512), F32),
         v((7, 128, 512), BF16),
         v((8, 256, 512), BF16), v((8, 256, 512), BF16), v((5, 256, 512), BF16),
         v((2, 256, 512), BF16),
         v((256, 512), BF16), v((256, 512), BF16), v((256, 512), BF16), v((2, 128, 512), BF16),
         v((256, 512), BF16), v((256, 512), BF16), v((256, 512), BF16),
-        v((512, GCOLS), BF16), v((512, half), BF16), v((4, 128, half), BF16), v((4, 32, half), BF16),
-        v((4, 32, half), BF16), v((32, half), BF16),
+        v((512, GCOLS), BF16), v((512, GCOLS), BF16),
+    ]
+    for _, _, columns, _ in PARTS:
+        half = columns // 2
+        scratch += [
+            v((512, half), BF16), v((4, 128, half), BF16), v((4, 32, half), BF16),
+            v((4, 32, half), BF16), v((32, half), BF16),
+        ]
+    scratch += [
+        pltpu.SemaphoreType.DMA((len(PARTS),)),
         pltpu.SemaphoreType.DMA((2,)),
         pltpu.SemaphoreType.DMA((N_SEM,)),
         pltpu.SemaphoreType.DMA((N_SEM,)),
@@ -528,17 +653,14 @@
             jax.ShapeDtypeStruct((512, GCOLS), BF16),
         ),
         in_specs=[smem, smem, smem, vmem, vmem, hbm, hbm],
-        out_specs=(vmem, vmem, vmem),
+        out_specs=(vmem, vmem, hbm),
         scratch_shapes=scratch,
         compiler_params=pltpu.CompilerParams(
             collective_id=0, has_side_effects=True, vmem_limit_bytes=56 * 2**20
         ),
         name="layer",
-    )(block_slots, pattern, lengths, events[0], upstream[0], in_weight, out_weight)
-    grad_in = jnp.concatenate(
-        [gw[:, g : g + 512] for g in (G_U, G_V, G_Q, G_K)], axis=1
-    ).astype(F32)
-    grad_out = gw[:, G_OUT : G_OUT + 512].astype(F32)
+    )(block_slots, pattern.T, lengths, events[0], upstream[0], in_weight, out_weight)
+    grad_in, grad_out, encoded, grad_events = finish(gw, encoded, grad_events)
     return encoded[None], grad_events[None], grad_in, grad_out
 
 

time: 105 us -> 76.1 us (0.72)
  Pallas kernels: 94.8 us -> 74.6 us
  other arithmetic: 5.53 us -> 0 us
  local copies, waits for them, and re-layouts: 2.78 us -> 0 us
    pallas_call x1, Pallas kernels: 94.8 us -> 70.8 us  [local(): pl.pallas_call(layer_kernel, out_shape=(jax.ShapeDtypeStruct((256, D), BF...]
    convert_element_type x2 -> x0, other arithmetic: 5.53 us -> none  [the longest x1 2.97 us: local(): grad_out = gw[:, G_OUT:G_OUT + 512].astype(F32)]
    pallas_call x0 -> x1, Pallas kernels: none -> 3.81 us  [finish(): pl.pallas_call(finish_kernel, out_shape=(jax.ShapeDtypeStruct((512, 2048)...]
    unnamed x7 -> x0, local copies, waits for them, and re-layouts: 2.78 us -> none
where the time goes in v2:
time: 76.1 us; the launch traced here: 75.9 us
  Pallas kernels  74.6 us (98%)
  between operations  1.29 us (2%)
    pallas_call x1, Pallas kernels, local(): pl.pallas_call(layer_kernel, out_shape=(jax.ShapeDtypeStruct((256, D), BF...  70.8 us
    pallas_call x1, Pallas kernels, finish(): pl.pallas_call(finish_kernel, out_shape=(jax.ShapeDtypeStruct((512, 2048)...  3.81 us

profile of v2, /device:TPU:1, one launch (start us, length us, event | category | flops | bytes accessed | tf_op | source)
XLA Modules:
  0.0 75.9 jit_solution(1270079970924603437)
XLA Ops:
  1.3 70.8 %layer.1 = (bf16[256,512]{1,0:T(8,128)(2,1)}, bf16[256,512]{1,0:T(8,128)(2,1)}, bf16[512,2560]{1,0:T(8,128)(2,1)}) custom-call(s32[32]{0:T(128)} %slots_ref.1, s32[3,32]{1,0:T(4,128)} %bitcast.7, s32[1]{0:T(128)S(6)} %copy.11.length_ref, bf16[256,512]{1,0:T(8,128)(2,1)} %bitcast.5, bf16[256,512]{1,0:T(8,128)(2,1)} %bitcast.6, bf16[512,2048]{1,0:T(8,128)(2,1)} %w_hbm.1, ...), custom_call_target="tpu_custom_call" | custom-call | tf_op jit(solution)/shard_map/layer/pallas_call | solution.py:648
  72.1 3.8 %finish.1 = (f32[512,2048]{1,0:T(8,128)}, f32[512,512]{1,0:T(8,128)}, bf16[256,512]{1,0:T(8,128)(2,1)}, bf16[256,512]{1,0:T(8,128)(2,1)}) custom-call(bf16[512,2560]{1,0:T(8,128)(2,1)} %get-tuple-element.11.gw, bf16[256,512]{1,0:T(8,128)(2,1)} %get-tuple-element.12.enc, bf16[256,512]{1,0:T(8,128)(2,1)} %get-tuple-element.13.gev), custom_call_target="tpu_custom_call" | custom-call | tf_op jit(solution)/shard_map/finish/pallas_call | solution.py:590

commit v3 on v2

--- a/solution.py
+++ b/solution.py
@@ -27,12 +27,13 @@
     ("q", G_Q, 512, ("z", "x", "y")),
 )
 SCHEDULE = (
-    "ou", "value_heads", "score_heads", "ou", "weight_k", "weight_q", "weight_v", "v", "q",
-    "k", "back_rows", "d2d_a", "q", "k", "v", "far_z", "far_y", "d2d_b",
-    "ou", "q", "k", "own_rows", "encode", "near_free", "last_own", "v", "ou",
-    "halves", "q", "v", "k", "near_z", "ou", "k", "ou", "q",
-    "near_tied", "v", "k", "q", "v", "k", "ou", "q", "k",
-    "v", "ou", "last", "q", "v",
+    "ou", "value_heads", "score_heads", "ou", "weight_k", "weight_q", "weight_v", "v",
+    "q", "k", "back_rows", "d2d_a", "q", "k", "v", "far_z0",
+    "far_z1", "far_y0", "far_y1", "d2d_b", "ou", "q", "k", "own_rows",
+    "encode", "near_free", "last_own", "v", "ou", "middle0", "middle1", "q",
+    "v", "k", "near_z0", "near_z1", "ou", "k", "ou", "q",
+    "near_p", "near_m", "v", "k", "q", "v", "k", "ou",
+    "q", "k", "v", "ou", "last", "q", "v",
 )
 
 
@@ -108,9 +109,9 @@
     grad_gated, limit_mask, weights, slope, mixed, grad_mixed, grad_q,
     gated, du, dq, dv, dk, own_grad, compact,
     to_sib, from_sib, sum_y, sum_z, r_z2, r_ya, r_yb, r_h, r_p, r_m, r_z0,
-    gp, gf, *rest,
+    gp, *rest,
 ):
-    ar_bufs, (ar_sems, w_sems, send_sems, recv_sems) = tuple(rest[:-4]), rest[-4:]
+    ar_bufs, (w_sems, send_sems, recv_sems) = rest[:-3], rest[-3:]
     dp = lax.axis_index("dp")
     ctx = lax.axis_index("ctx")
     x, zh = dp // 2, dp % 2
@@ -331,7 +332,7 @@
         return sum(part.astype(F32) for part in parts).astype(BF16)
 
     def reduce_columns(lo, n, axes, bufs):
-        sibling, first, second, third, total, local_sem = bufs
+        sibling, first, second, third, total = bufs
         a1, a2, a3 = axes
         p1, p2, p3 = (place[a] for a in axes)
         half = n // 2
@@ -371,17 +372,15 @@
         yield
         for at, i in zip(ats, near_first):
             net.landed(at, third.at[rot(p3, i)])
-        gf[rows2(p2), mine] = add4([third[0], third[1], third[2], third[3]])
-        here = gf.at[rows2(p2), mine]
+        gw[rows2(p2), mine] = add4([third[0], third[1], third[2], third[3]])
+        here = gw.at[rows2(p2), mine]
         ats = [net.send(here, here, rings[a2][i]) for i in far_first]
         yield
         for at, i in zip(ats, near_first):
-            net.landed(at, gf.at[rows2(rot(p2, i)), mine])
-        here, there = gf.at[rows1(p1), mine], gw.at[rows1(p1), mine]
-        ats = [net.send(here, there, rings[a1][i]) for i in far_first]
-        back = [net.send(here, there, sib)]
-        keep = pltpu.make_async_copy(here, there, local_sem)
-        keep.start()
+            net.landed(at, gw.at[rows2(rot(p2, i)), mine])
+        here = gw.at[rows1(p1), mine]
+        ats = [net.send(here, here, rings[a1][i]) for i in far_first]
+        back = [net.send(here, here, sib)]
         yield
         for at, i in zip(ats, near_first):
             there = gw.at[rows1(rot(p1, i)), mine]
@@ -390,11 +389,10 @@
         yield
         for at, i in zip(back, (0,) + near_first):
             net.landed(at, gw.at[rows1(rot(p1, i)), other])
-        keep.wait()
         yield
 
     parts = {
-        name: reduce_columns(lo, n, axes, ar_bufs[5 * i : 5 * i + 5] + (ar_sems.at[i],))
+        name: reduce_columns(lo, n, axes, ar_bufs[5 * i : 5 * i + 5])
         for i, (name, lo, n, axes) in enumerate(PARTS)
     }
 
@@ -496,35 +494,33 @@
     def d2d_b():
         to_sibling(((0, 2), (1, 0), (0, 1), (0, 3), (0, 0)))
 
-    def far_z():
-        for half in range(2):
-            pass_on("z2", sum_z.at[0], 1, 2, half, r_z2.at[HALF[half]], zp)
-
-    def far_y():
-        for half in range(2):
-            pass_on("ya", sum_y.at[0], 1, 1, half, r_ya.at[HALF[half]], yp)
-            pass_on("yb", sum_y.at[1], 1, 3, half, r_yb.at[HALF[half]], ym)
+    def far_z(half):
+        pass_on("z2", sum_z.at[0], 1, 2, half, r_z2.at[HALF[half]], zp)
+
+    def far_y(half):
+        pass_on("ya", sum_y.at[0], 1, 1, half, r_ya.at[HALF[half]], yp)
+        pass_on("yb", sum_y.at[1], 1, 3, half, r_yb.at[HALF[half]], ym)
 
     def near_free():
         pass_on("p", sum_y.at[3], 0, 1, 1, r_p.at[HALF[1]], yp)
         pass_on("m", sum_y.at[4], 0, 3, 0, r_m.at[HALF[0]], ym)
 
-    def halves():
-        for half in range(2):
-            pass_on(
-                "h", sum_y.at[2], 0, 2, half, r_h.at[half], (yp, ym)[half],
-                (("z2", r_z2.at[HALF[half]]),),
-            )
-
-    def near_z():
-        for half in range(2):
-            pass_on(
-                "z0", sum_z.at[1], 1, 0, half, r_z0.at[HALF[half]], zp,
-                (("ya", r_ya.at[HALF[half]]), ("yb", r_yb.at[HALF[half]])),
-            )
-
-    def near_tied():
+    def middle(half):
+        pass_on(
+            "h", sum_y.at[2], 0, 2, half, r_h.at[half], (yp, ym)[half],
+            (("z2", r_z2.at[HALF[half]]),),
+        )
+
+    def near_z(half):
+        pass_on(
+            "z0", sum_z.at[1], 1, 0, half, r_z0.at[HALF[half]], zp,
+            (("ya", r_ya.at[HALF[half]]), ("yb", r_yb.at[HALF[half]])),
+        )
+
+    def near_p():
         pass_on("p", sum_y.at[3], 0, 1, 0, r_p.at[HALF[0]], yp, (("h", r_h.at[0]),))
+
+    def near_m():
         pass_on("m", sum_y.at[4], 0, 3, 1, r_m.at[HALF[1]], ym, (("h", r_h.at[1]),))
 
     def last_own():
@@ -545,9 +541,12 @@
     steps = dict(
         value_heads=value_heads, weight_v=weight_v, score_heads=score_heads, weight_k=weight_k,
         weight_q=weight_q, back_rows=back_rows, encode=encode, own_rows=own_rows, d2d_a=d2d_a,
-        d2d_b=d2d_b, far_z=far_z, far_y=far_y, near_free=near_free, halves=halves,
-        near_z=near_z, near_tied=near_tied, last_own=last_own, last=last,
+        d2d_b=d2d_b, near_free=near_free, near_p=near_p, near_m=near_m, last_own=last_own,
+        last=last,
     )
+    for half in range(2):
+        for step in (far_z, far_y, middle, near_z):
+            steps[step.__name__ + str(half)] = functools.partial(step, half)
     for step in SCHEDULE:
         if step in parts:
             next(parts[step])
@@ -556,37 +555,29 @@
     net.drain()
 
 
-def finish_kernel(
-    gw, enc, gev, grad_in, grad_out, encoded, grad_events, got, full, rest, in_sems, out_sems
-):
-    rows = [pl.ds(i * 128, 128) for i in range(4)]
-    reads = [pltpu.make_async_copy(gw.at[r], got.at[r], in_sems.at[i]) for i, r in enumerate(rows)]
-    reads += [
-        pltpu.make_async_copy(enc, rest.at[0], in_sems.at[4]),
-        pltpu.make_async_copy(gev, rest.at[1], in_sems.at[5]),
+def finish_kernel(gw, enc, gev, grad_in, grad_out, encoded, grad_events, full, sems):
+    writes = [
+        pltpu.make_async_copy(enc, encoded, sems.at[8]),
+        pltpu.make_async_copy(gev, grad_events, sems.at[9]),
     ]
-    for copy in reads:
-        copy.start()
-    writes = []
-    for i, r in enumerate(rows):
-        reads[i].wait()
-        full[r, :] = got[r, :].astype(F32)
+    for i in range(4):
+        rows = pl.ds(i * 128, 128)
+        full[rows, :] = gw[rows, :].astype(F32)
         writes += [
-            pltpu.make_async_copy(full.at[r, pl.ds(512, 2048)], grad_in.at[r], out_sems.at[i]),
-            pltpu.make_async_copy(full.at[r, pl.ds(0, 512)], grad_out.at[r], out_sems.at[4 + i]),
+            pltpu.make_async_copy(full.at[rows, pl.ds(512, 2048)], grad_in.at[rows], sems.at[i]),
+            pltpu.make_async_copy(full.at[rows, pl.ds(0, 512)], grad_out.at[rows], sems.at[4 + i]),
         ]
         for copy in writes[-2:]:
             copy.start()
-    for i, (copy, out) in enumerate(zip(reads[4:], (encoded, grad_events))):
-        copy.wait()
-        writes.append(pltpu.make_async_copy(rest.at[i], out, out_sems.at[8 + i]))
-        writes[-1].start()
+    for copy in writes[:2]:
+        copy.start()
     for copy in writes:
         copy.wait()
 
 
 def finish(gw, enc, gev):
     hbm = pl.BlockSpec(memory_space=pl.ANY)
+    vmem = pl.BlockSpec(memory_space=pltpu.VMEM)
     return pl.pallas_call(
         finish_kernel,
         out_shape=(
@@ -595,16 +586,10 @@
             jax.ShapeDtypeStruct((256, D), BF16),
             jax.ShapeDtypeStruct((256, D), BF16),
         ),
-        in_specs=[hbm] * 3,
+        in_specs=[vmem] * 3,
         out_specs=(hbm,) * 4,
-        scratch_shapes=[
-            pltpu.VMEM((512, GCOLS), BF16),
-            pltpu.VMEM((512, GCOLS), F32),
-            pltpu.VMEM((2, 256, D), BF16),
-            pltpu.SemaphoreType.DMA((6,)),
-            pltpu.SemaphoreType.DMA((10,)),
-        ],
-        compiler_params=pltpu.CompilerParams(vmem_limit_bytes=60 * 2**20),
+        scratch_shapes=[pltpu.VMEM((512, GCOLS), F32), pltpu.SemaphoreType.DMA((10,))],
+        compiler_params=pltpu.CompilerParams(vmem_limit_bytes=24 * 2**20),
         name="finish",
     )(gw, enc, gev)
 
@@ -631,7 +616,7 @@
         v((2, 256, 512), BF16),
         v((256, 512), BF16), v((256, 512), BF16), v((256, 512), BF16), v((2, 128, 512), BF16),
         v((256, 512), BF16), v((256, 512), BF16), v((256, 512), BF16),
-        v((512, GCOLS), BF16), v((512, GCOLS), BF16),
+        v((512, GCOLS), BF16),
     ]
     for _, _, columns, _ in PARTS:
         half = columns // 2
@@ -640,7 +625,6 @@
             v((4, 32, half), BF16), v((32, half), BF16),
         ]
     scratch += [
-        pltpu.SemaphoreType.DMA((len(PARTS),)),
         pltpu.SemaphoreType.DMA((2,)),
         pltpu.SemaphoreType.DMA((N_SEM,)),
         pltpu.SemaphoreType.DMA((N_SEM,)),
@@ -648,15 +632,15 @@
     encoded, grad_events, gw = pl.pallas_call(
         layer_kernel,
         out_shape=(
-            jax.ShapeDtypeStruct((256, D), BF16),
-            jax.ShapeDtypeStruct((256, D), BF16),
-            jax.ShapeDtypeStruct((512, GCOLS), BF16),
+            pltpu.VMEM((256, D), BF16),
+            pltpu.VMEM((256, D), BF16),
+            pltpu.VMEM((512, GCOLS), BF16),
         ),
         in_specs=[smem, smem, smem, vmem, vmem, hbm, hbm],
-        out_specs=(vmem, vmem, hbm),
+        out_specs=(vmem, vmem, vmem),
         scratch_shapes=scratch,
         compiler_params=pltpu.CompilerParams(
-            collective_id=0, has_side_effects=True, vmem_limit_bytes=56 * 2**20
+            collective_id=0, has_side_effects=True, vmem_limit_bytes=54 * 2**20
         ),
         name="layer",
     )(block_slots, pattern.T, lengths, events[0], upstream[0], in_weight, out_weight)

time: 76.1 us -> 73.6 us (0.967)
  Pallas kernels: 74.6 us -> 72.2 us
    pallas_call x1, Pallas kernels: 70.8 us -> 69.5 us  [local(): pl.pallas_call(layer_kernel, out_shape=(pltpu.VMEM((256, D), BF16), pltpu...]
    pallas_call x1, Pallas kernels: 3.81 us -> 2.68 us  [finish(): pl.pallas_call(finish_kernel, out_shape=(jax.ShapeDtypeStruct((512, 2048)...]
where the time goes in v3:
time: 73.6 us; the launch traced here: 73.5 us
  Pallas kernels  72.2 us (98%)
  between operations  1.29 us (2%)
    pallas_call x1, Pallas kernels, local(): pl.pallas_call(layer_kernel, out_shape=(pltpu.VMEM((256, D), BF16), pltpu...  69.5 us
    pallas_call x1, Pallas kernels, finish(): pl.pallas_call(finish_kernel, out_shape=(jax.ShapeDtypeStruct((512, 2048)...  2.68 us

profile of v3, /device:TPU:1, one launch (start us, length us, event | category | flops | bytes accessed | tf_op | source)
XLA Modules:
  0.0 73.5 jit_solution(4257701271935540767)
XLA Ops:
  1.3 69.5 %layer.1 = (bf16[256,512]{1,0:T(8,128)(2,1)S(1)}, bf16[256,512]{1,0:T(8,128)(2,1)S(1)}, bf16[512,2560]{1,0:T(8,128)(2,1)S(1)}) custom-call(s32[32]{0:T(128)} %slots_ref.1, s32[3,32]{1,0:T(4,128)} %bitcast.7, s32[1]{0:T(128)S(6)} %copy.11.length_ref, bf16[256,512]{1,0:T(8,128)(2,1)} %bitcast.5, bf16[256,512]{1,0:T(8,128)(2,1)} %bitcast.6, ...), custom_call_target="tpu_custom_call" | custom-call | tf_op jit(solution)/shard_map/layer/pallas_call | solution.py:632
  70.8 2.7 %finish.1 = (f32[512,2048]{1,0:T(8,128)}, f32[512,512]{1,0:T(8,128)}, bf16[256,512]{1,0:T(8,128)(2,1)}, bf16[256,512]{1,0:T(8,128)(2,1)}) custom-call(bf16[512,2560]{1,0:T(8,128)(2,1)S(1)} %get-tuple-element.11.gw, bf16[256,512]{1,0:T(8,128)(2,1)S(1)} %get-tuple-element.12.enc, bf16[256,512]{1,0:T(8,128)(2,1)S(1)} %get-tuple-element.13.gev), custom_call_target="tpu_custom_call" | custom-call | tf_op jit(solution)/shard_map/finish/pallas_call | solution.py:581

commit v4 on v3

--- a/solution.py
+++ b/solution.py
@@ -21,19 +21,22 @@
 GCOLS = 2560
 N_SEM = 176
 PARTS = (
-    ("ou", G_OUT, 1024, ("y", "x", "z")),
-    ("v", G_V, 512, ("x", "z", "y")),
+    ("a", G_OUT, 512, ("x", "y", "z")),
+    ("b", G_U, 256, ("y", "z", "x")),
+    ("c", G_U + 256, 256, ("z", "x", "y")),
+    ("v", G_V, 512, ("z", "x", "y")),
+    ("q", G_Q, 512, ("y", "z", "x")),
     ("k", G_K, 512, ("x", "y", "z")),
-    ("q", G_Q, 512, ("z", "x", "y")),
 )
 SCHEDULE = (
-    "ou", "value_heads", "score_heads", "ou", "weight_k", "weight_q", "weight_v", "v",
-    "q", "k", "back_rows", "d2d_a", "q", "k", "v", "far_z0",
-    "far_z1", "far_y0", "far_y1", "d2d_b", "ou", "q", "k", "own_rows",
-    "encode", "near_free", "last_own", "v", "ou", "middle0", "middle1", "q",
-    "v", "k", "near_z0", "near_z1", "ou", "k", "ou", "q",
-    "near_p", "near_m", "v", "k", "q", "v", "k", "ou",
-    "q", "k", "v", "ou", "last", "q", "v",
+    "score_heads", "weight_k", "c", "weight_q", "q", "k", "a", "b", "value_heads",
+    "weight_v", "c", "v", "k", "b", "v", "a", "q", "back_rows",
+    "d2d_a", "c", "d2d_b", "own_rows", "b", "k", "far_z1", "far_y0", "v",
+    "q", "a", "k", "far_z0", "c", "near_free", "v", "near_z0", "q",
+    "a", "k", "middle1", "c", "b", "last_own", "far_y1", "encode", "q",
+    "middle0", "v", "b", "c", "k", "a", "b", "v", "q",
+    "c", "near_z1", "k", "a", "near_p", "c", "near_m", "b", "k",
+    "b", "v", "q", "v", "a", "last", "q", "a",
 )
 
 
@@ -102,16 +105,31 @@
 
 
 def layer_kernel(
-    slots_ref, pattern_ref, length_ref, events, upstream, w_hbm, wo_hbm,
-    encoded, grad_events, gw,
-    w, wo, gx, normed, own_normed, hat_in, inv_in,
-    u_act, u_slope, q_act, q_slope, k_act, k_slope, v_act, v_slope,
-    grad_gated, limit_mask, weights, slope, mixed, grad_mixed, grad_q,
-    gated, du, dq, dv, dk, own_grad, compact,
-    to_sib, from_sib, sum_y, sum_z, r_z2, r_ya, r_yb, r_h, r_p, r_m, r_z0,
-    gp, *rest,
+    slots_ref, pattern_ref, length_ref, events_hbm, upstream_hbm, w_hbm, wo_hbm,
+    encoded, grad_events, *rest,
 ):
-    ar_bufs, (w_sems, send_sems, recv_sems) = rest[:-3], rest[-3:]
+    outs, rest = rest[: len(PARTS)], rest[len(PARTS) :]
+    (
+        w, wo, gx, normed, own_normed, hat_in, inv_in, u_act,
+        u_slope, q_act, q_slope, k_act, k_slope, v_act, v_slope, grad_gated,
+        limit_mask, weights, slope, mixed, grad_mixed, grad_q, gated, du,
+        dq, dv, dk, own_grad, compact, to_sib, from_sib, sum_y,
+        sum_z, r_z2, r_ya, r_yb, r_h, r_p, r_m, r_z0,
+        events, upstream,
+    ) = rest[:42]
+    ar_bufs, (in_sems, send_sems, recv_sems) = rest[42:-3], rest[-3:]
+
+    def part_bufs(i):
+        return (ar_bufs[6 * i], outs[i], *ar_bufs[6 * i + 1 : 6 * i + 6])
+
+    def store_columns(lo, values):
+        for at in range(lo, lo + values.shape[1], 128):
+            for i, (_, start, n, _) in enumerate(PARTS):
+                if start <= at < start + n:
+                    half = n // 2
+                    c, off = (at - start) // half, (at - start) % half
+                    part_bufs(i)[0][c, :, off : off + 128] = values[:, at - lo : at - lo + 128]
+
     dp = lax.axis_index("dp")
     ctx = lax.axis_index("ctx")
     x, zh = dp // 2, dp % 2
@@ -131,15 +149,20 @@
     ring_y = [dev(x, rot(y, i), z, core) for i in range(4)]
     ring_z = [dev(x, y, rot(z, i), core) for i in range(4)]
 
-    w_copy = pltpu.make_async_copy(w_hbm, w, w_sems.at[0])
-    wo_copy = pltpu.make_async_copy(wo_hbm, wo, w_sems.at[1])
-    w_copy.start()
-    wo_copy.start()
-
     barrier = pltpu.get_barrier_semaphore()
-    partners = [sib] + ring_x[1:] + ring_y[1:] + ring_z[1:]
+    partners = [sib, yp, ym] + ring_z[1:] + [y2] + ring_x[1:]
     for partner in partners:
         pl.semaphore_signal(barrier, inc=1, device_id=partner, device_id_type=MESH)
+
+    loads = [
+        pltpu.make_async_copy(src, dst, in_sems.at[i])
+        for i, (src, dst) in enumerate(
+            ((events_hbm, events), (upstream_hbm, upstream), (w_hbm, w), (wo_hbm, wo))
+        )
+    ]
+    for copy in loads:
+        copy.start()
+    loads[0].wait()
 
     net = Net(send_sems, recv_sems)
 
@@ -176,8 +199,8 @@
     own_normed[...] = own
     for b in range(2):
         normed[b * 512 : b * 512 + 128, :] = own[b * 128 : b * 128 + 128]
-    w_copy.wait()
-    wo_copy.wait()
+    for copy in loads[1:]:
+        copy.wait()
 
     def activate(pre):
         sig = sigmoid(pre)
@@ -265,13 +288,16 @@
     net.landed(f_ym1, rows(1, 1, 0, 1))
     d6 = forward(rows(1, 1), sib)
     net.landed(z2_0, rows(1, 2, 0, 0))
+    d7 = forward(rows(1, 2, 0, 0), sib)
     net.landed(z2_1, rows(1, 2, 0, 1))
-    d7 = forward(rows(1, 2), sib)
+    d8 = forward(rows(1, 2, 0, 1), sib)
     for at, (dz, dy) in zip(
-        (a_sib, d1, d2, d3, d4, d5, d6, d7),
-        ((0, 0), (0, 3), (0, 1), (1, 0), (0, 2), (1, 3), (1, 1), (1, 2)),
+        (a_sib, d1, d2, d3, d4, d5, d6),
+        ((0, 0), (0, 3), (0, 1), (1, 0), (0, 2), (1, 3), (1, 1)),
     ):
         net.landed(at, rows(dz, dy, 1))
+    net.landed(d7, rows(1, 2, 1, 0))
+    net.landed(d8, rows(1, 2, 1, 1))
 
     for b in range(2):
         for t in range(1, 4):
@@ -285,14 +311,12 @@
     def forward_head(i, carry):
         b, h = i // 4, i % 4
         q = q_act[h, pl.ds(pl.multiple_of(b * 128, 128), 128), :]
-        for t in range(4):
-            lo = pl.multiple_of(b * 512 + t * 128, 128)
-            s = dot_nt(q, k_act[h, pl.ds(lo, 128), :]) * SCALE
-            mask = limit_mask[b, :, t * 128 : t * 128 + 128]
-            sig = sigmoid(s)
-            act = s * sig
-            weights[i, :, t * 128 : t * 128 + 128] = (act * mask).astype(BF16)
-            slope[i, :, t * 128 : t * 128 + 128] = (sig + act * (1.0 - sig)) * (mask * SCALE)
+        s = dot_nt(q, k_act[h, pl.ds(pl.multiple_of(b * 512, 512), 512), :]) * SCALE
+        mask = limit_mask[b]
+        sig = sigmoid(s)
+        act = s * sig
+        weights[i] = (act * mask).astype(BF16)
+        slope[i] = (sig + act * (1.0 - sig)) * (mask * SCALE)
         mixed[h, pl.ds(pl.multiple_of(b * 128, 128), 128), :] = dot(
             weights[i], v_act[h, pl.ds(pl.multiple_of(b * 512, 512), 512), :]
         )
@@ -319,8 +343,8 @@
     mean_th = across([ts[h] * hats[h] for h in range(4)])
     for h in range(4):
         grad_mixed[h] = (inv_mix * (ts[h] - mean_t - hats[h] * mean_th)).astype(BF16)
-    gp[:, G_OUT : G_OUT + 512] = dot_tn(gated[...], upstream[...]).astype(BF16)
-    gp[:, G_U : G_U + 512] = dot_tn(own_normed[...], du[...]).astype(BF16)
+    store_columns(G_OUT, dot_tn(gated[...], upstream[...]).astype(BF16))
+    store_columns(G_U, dot_tn(own_normed[...], du[...]).astype(BF16))
 
     place = {"x": x, "y": y, "z": z}
     rings = {"x": ring_x, "y": ring_y, "z": ring_z}
@@ -332,13 +356,10 @@
         return sum(part.astype(F32) for part in parts).astype(BF16)
 
     def reduce_columns(lo, n, axes, bufs):
-        sibling, first, second, third, total = bufs
+        gp, gw, sibling, first, second, third, total = bufs
         a1, a2, a3 = axes
         p1, p2, p3 = (place[a] for a in axes)
-        half = n // 2
-        mine = pl.ds(pl.multiple_of(lo + core * half, 128), half)
-        other = pl.ds(pl.multiple_of(lo + (1 - core) * half, 128), half)
-        far_first, near_first = (1, 3, 2), (3, 1, 2)
+        far_first, near_first = (2, 1, 3), (2, 3, 1)
 
         def rows1(p):
             return span(p * 128, 128)
@@ -346,13 +367,13 @@
         def rows2(p):
             return span(p1 * 128 + p * 32, 32)
 
-        at = net.send(gp.at[:, other], sibling, sib)
+        at = net.send(gp.at[1 - core], sibling, sib)
         yield
         net.landed(at, sibling)
         ats = []
         for i in far_first + (0,):
             block = rows1(rot(p1, i))
-            sibling[block, :] = gp[block, mine] + sibling[block, :]
+            sibling[block, :] = gp[core, block, :] + sibling[block, :]
             if i:
                 ats.append(net.send(sibling.at[block], first.at[i], rings[a1][i]))
         yield
@@ -372,27 +393,27 @@
         yield
         for at, i in zip(ats, near_first):
             net.landed(at, third.at[rot(p3, i)])
-        gw[rows2(p2), mine] = add4([third[0], third[1], third[2], third[3]])
-        here = gw.at[rows2(p2), mine]
+        gw[core, rows2(p2), :] = add4([third[0], third[1], third[2], third[3]])
+        here = gw.at[core, rows2(p2)]
         ats = [net.send(here, here, rings[a2][i]) for i in far_first]
         yield
         for at, i in zip(ats, near_first):
-            net.landed(at, gw.at[rows2(rot(p2, i)), mine])
-        here = gw.at[rows1(p1), mine]
+            net.landed(at, gw.at[core, rows2(rot(p2, i))])
+        here = gw.at[core, rows1(p1)]
         ats = [net.send(here, here, rings[a1][i]) for i in far_first]
         back = [net.send(here, here, sib)]
         yield
         for at, i in zip(ats, near_first):
-            there = gw.at[rows1(rot(p1, i)), mine]
+            there = gw.at[core, rows1(rot(p1, i))]
             net.landed(at, there)
             back.append(net.send(there, there, sib))
         yield
         for at, i in zip(back, (0,) + near_first):
-            net.landed(at, gw.at[rows1(rot(p1, i)), other])
+            net.landed(at, gw.at[1 - core, rows1(rot(p1, i))])
         yield
 
     parts = {
-        name: reduce_columns(lo, n, axes, ar_bufs[5 * i : 5 * i + 5])
+        name: reduce_columns(lo, n, axes, part_bufs(i))
         for i, (name, lo, n, axes) in enumerate(PARTS)
     }
 
@@ -410,7 +431,7 @@
         lax.fori_loop(0, 8, value_head, 0, unroll=8)
 
     def weight_v():
-        gp[:, G_V : G_V + 512] = dot_tn(normed[...], heads_of(dv)).astype(BF16)
+        store_columns(G_V, dot_tn(normed[...], heads_of(dv)).astype(BF16))
 
     def score_head(i, carry):
         b, h = i // 4, i % 4
@@ -427,13 +448,13 @@
         lax.fori_loop(0, 8, score_head, 0, unroll=8)
 
     def weight_k():
-        gp[:, G_K : G_K + 512] = dot_tn(normed[...], heads_of(dk)).astype(BF16)
+        store_columns(G_K, dot_tn(normed[...], heads_of(dk)).astype(BF16))
 
     def weight_q():
         dq[...] = jnp.concatenate(
             [(grad_q[h] * q_slope[h]).astype(BF16) for h in range(4)], axis=1
         )
-        gp[:, G_Q : G_Q + 512] = dot_tn(own_normed[...], dq[...]).astype(BF16)
+        store_columns(G_Q, dot_tn(own_normed[...], dq[...]).astype(BF16))
 
     def back_rows():
         back = dot_nt(heads_of(dv), w[:, 512:1024]) + dot_nt(heads_of(dk), w[:, 1536:2048])
@@ -555,14 +576,18 @@
     net.drain()
 
 
-def finish_kernel(gw, enc, gev, grad_in, grad_out, encoded, grad_events, full, sems):
+def finish_kernel(enc, gev, *refs):
+    gws, (grad_in, grad_out, encoded, grad_events, full, sems) = refs[:-6], refs[-6:]
     writes = [
         pltpu.make_async_copy(enc, encoded, sems.at[8]),
         pltpu.make_async_copy(gev, grad_events, sems.at[9]),
     ]
     for i in range(4):
         rows = pl.ds(i * 128, 128)
-        full[rows, :] = gw[rows, :].astype(F32)
+        for gw, (_, lo, n, _) in zip(gws, PARTS):
+            half = n // 2
+            for c in range(2):
+                full[rows, lo + c * half : lo + c * half + half] = gw[c, rows, :].astype(F32)
         writes += [
             pltpu.make_async_copy(full.at[rows, pl.ds(512, 2048)], grad_in.at[rows], sems.at[i]),
             pltpu.make_async_copy(full.at[rows, pl.ds(0, 512)], grad_out.at[rows], sems.at[4 + i]),
@@ -586,12 +611,12 @@
             jax.ShapeDtypeStruct((256, D), BF16),
             jax.ShapeDtypeStruct((256, D), BF16),
         ),
-        in_specs=[vmem] * 3,
+        in_specs=[vmem] * (2 + len(gw)),
         out_specs=(hbm,) * 4,
         scratch_shapes=[pltpu.VMEM((512, GCOLS), F32), pltpu.SemaphoreType.DMA((10,))],
         compiler_params=pltpu.CompilerParams(vmem_limit_bytes=24 * 2**20),
         name="finish",
-    )(gw, enc, gev)
+    )(enc, gev, *gw)
 
 
 def local(events, upstream, lengths, block_slots, pattern, in_weight, out_weight):
@@ -616,28 +641,28 @@
         v((2, 256, 512), BF16),
         v((256, 512), BF16), v((256, 512), BF16), v((256, 512), BF16), v((2, 128, 512), BF16),
         v((256, 512), BF16), v((256, 512), BF16), v((256, 512), BF16),
-        v((512, GCOLS), BF16),
+        v((256, 512), BF16), v((256, 512), BF16),
     ]
     for _, _, columns, _ in PARTS:
         half = columns // 2
         scratch += [
-            v((512, half), BF16), v((4, 128, half), BF16), v((4, 32, half), BF16),
+            v((2, 512, half), BF16), v((512, half), BF16), v((4, 128, half), BF16), v((4, 32, half), BF16),
             v((4, 32, half), BF16), v((32, half), BF16),
         ]
     scratch += [
-        pltpu.SemaphoreType.DMA((2,)),
+        pltpu.SemaphoreType.DMA((4,)),
         pltpu.SemaphoreType.DMA((N_SEM,)),
         pltpu.SemaphoreType.DMA((N_SEM,)),
     ]
-    encoded, grad_events, gw = pl.pallas_call(
+    encoded, grad_events, *gw = pl.pallas_call(
         layer_kernel,
         out_shape=(
             pltpu.VMEM((256, D), BF16),
             pltpu.VMEM((256, D), BF16),
-            pltpu.VMEM((512, GCOLS), BF16),
+            *[pltpu.VMEM((2, 512, n // 2), BF16) for _, _, n, _ in PARTS],
         ),
-        in_specs=[smem, smem, smem, vmem, vmem, hbm, hbm],
-        out_specs=(vmem, vmem, vmem),
+        in_specs=[smem, smem, smem, hbm, hbm, hbm, hbm],
+        out_specs=(vmem,) * (2 + len(PARTS)),
         scratch_shapes=scratch,
         compiler_params=pltpu.CompilerParams(
             collective_id=0, has_side_effects=True, vmem_limit_bytes=54 * 2**20

time: 73.6 us -> 72.5 us (0.985)
  Pallas kernels: 72.2 us -> 71 us
    pallas_call x1, Pallas kernels: 69.5 us -> 68.3 us  [local(): pl.pallas_call(layer_kernel, out_shape=(pltpu.VMEM((256, D), BF16), pltpu...]
where the time goes in v4:
time: 72.5 us; the launch traced here: 72.3 us
  Pallas kernels  71 us (98%)
  between operations  1.29 us (2%)
    pallas_call x1, Pallas kernels, local(): pl.pallas_call(layer_kernel, out_shape=(pltpu.VMEM((256, D), BF16), pltpu...  68.3 us
    pallas_call x1, Pallas kernels, finish(): pl.pallas_call(finish_kernel, out_shape=(jax.ShapeDtypeStruct((512, 2048)...  2.69 us

profile of v4, /device:TPU:1, one launch (start us, length us, event | category | flops | bytes accessed | tf_op | source)
XLA Modules:
  0.0 72.3 jit_solution(1571879992574197356)
XLA Ops:
  1.3 68.3 %layer.1 = (bf16[256,512]{1,0:T(8,128)(2,1)S(1)}, bf16[256,512]{1,0:T(8,128)(2,1)S(1)}, bf16[2,512,256]{2,1,0:T(8,128)(2,1)S(1)}, bf16[2,512,128]{2,1,0:T(8,128)...) custom-call(s32[32]{0:T(128)} %slots_ref.1, ...), custom_call_target="tpu_custom_call" | custom-call | tf_op jit(solution)/shard_map/layer/pallas_call | solution.py:657
  69.6 2.7 %finish.1 = (f32[512,2048]{1,0:T(8,128)}, f32[512,512]{1,0:T(8,128)}, bf16[256,512]{1,0:T(8,128)(2,1)}, bf16[256,512]{1,0:T(8,128)(2,1)}) custom-call(bf16[256,512]{1,0:T(8,128)(2,1)S(1)} %get-tuple-element.16.enc, bf16[256,512]{1,0:T(8,128)(2,1)S(1)} %get-tuple-element.17.gev, bf16[2,512,256]{2,1,0:T(8,128)(2,1)S(1)} %get-tuple-element.18.refs_0_, ...), custom_call_target="tpu_custom_call" | custom-call | tf_op jit(solution)/shard_map/finish/pallas_call | solution.py:606

commit v5 on v4

--- a/solution.py
+++ b/solution.py
@@ -160,9 +160,6 @@
             ((events_hbm, events), (upstream_hbm, upstream), (w_hbm, w), (wo_hbm, wo))
         )
     ]
-    for copy in loads:
-        copy.start()
-    loads[0].wait()
 
     net = Net(send_sems, recv_sems)
 
@@ -177,8 +174,18 @@
             return gx.at[pl.ds(base, 2)]
         return gx.at[base + half]
 
-    for half in range(2):
-        gx[shard(0, 0, 0) + half] = events[half * 128 : half * 128 + 128, :]
+    first_rows = [
+        pltpu.make_async_copy(
+            events_hbm.at[pl.ds(half * 128, 128)],
+            gx.at[shard(0, 0, 0) + half],
+            in_sems.at[4 + half],
+        )
+        for half in range(2)
+    ]
+    for copy in first_rows + loads:
+        copy.start()
+    for copy in first_rows:
+        copy.wait()
     pl.semaphore_wait(barrier, len(partners))
 
     def forward(ref, device):
@@ -192,6 +199,8 @@
     a_ym1 = forward(rows(0, 0, 0, 0), ym)
     a_z1 = forward(rows(0, 0, 0, 1), zp)
 
+    for copy in loads:
+        copy.wait()
     hat, inv = norm_rows(events[...].astype(F32))
     hat_in[...] = hat
     inv_in[...] = inv
@@ -199,8 +208,6 @@
     own_normed[...] = own
     for b in range(2):
         normed[b * 512 : b * 512 + 128, :] = own[b * 128 : b * 128 + 128]
-    for copy in loads[1:]:
-        copy.wait()
 
     def activate(pre):
         sig = sigmoid(pre)
@@ -650,7 +657,7 @@
             v((4, 32, half), BF16), v((32, half), BF16),
         ]
     scratch += [
-        pltpu.SemaphoreType.DMA((4,)),
+        pltpu.SemaphoreType.DMA((6,)),
         pltpu.SemaphoreType.DMA((N_SEM,)),
         pltpu.SemaphoreType.DMA((N_SEM,)),
     ]

time: 72.5 us -> 72.5 us (level)
  no operation moved by 1% of the time
where the time goes in v5:
time: 72.5 us; the launch traced here: 72.3 us
  Pallas kernels  71 us (98%)
  between operations  1.29 us (2%)
    pallas_call x1, Pallas kernels, local(): pl.pallas_call(layer_kernel, out_shape=(pltpu.VMEM((256, D), BF16), pltpu...  68.3 us
    pallas_call x1, Pallas kernels, finish(): pl.pallas_call(finish_kernel, out_shape=(jax.ShapeDtypeStruct((512, 2048)...  2.69 us

profile of v5, /device:TPU:1, one launch (start us, length us, event | category | flops | bytes accessed | tf_op | source)
XLA Modules:
  0.0 72.3 jit_solution(2510831173209665997)
XLA Ops:
  1.3 68.3 %layer.1 = (bf16[256,512]{1,0:T(8,128)(2,1)S(1)}, bf16[256,512]{1,0:T(8,128)(2,1)S(1)}, bf16[2,512,256]{2,1,0:T(8,128)(2,1)S(1)}, bf16[2,512,128]{2,1,0:T(8,128)...) custom-call(s32[32]{0:T(128)} %slots_ref.1, ...), custom_call_target="tpu_custom_call" | custom-call | tf_op jit(solution)/shard_map/layer/pallas_call | solution.py:664
  69.6 2.7 %finish.1 = (f32[512,2048]{1,0:T(8,128)}, f32[512,512]{1,0:T(8,128)}, bf16[256,512]{1,0:T(8,128)(2,1)}, bf16[256,512]{1,0:T(8,128)(2,1)}) custom-call(bf16[256,512]{1,0:T(8,128)(2,1)S(1)} %get-tuple-element.16.enc, bf16[256,512]{1,0:T(8,128)(2,1)S(1)} %get-tuple-element.17.gev, bf16[2,512,256]{2,1,0:T(8,128)(2,1)S(1)} %get-tuple-element.18.refs_0_, ...), custom_call_target="tpu_custom_call" | custom-call | tf_op jit(solution)/shard_map/finish/pallas_call | solution.py:613
